TPU v7x, 512 devices: a whole 4x8x8 slice. The times are simulated.
512 devices in a mesh: row: 32 (over x, z), height: 16 (over y, core).
Axes of the slice: x: 4, y: 8, z: 8, core: 2. Of those that a mesh axis runs over, the one named last changes fastest.
Arguments:
- streamwise_wind_edges: float32 [256, 32, 4096], P('height', None, 'row'), may hold values from -6 to 6
- climbing_wind_edges: float32 [256, 32, 4096], P('height', None, 'row'), may hold values from -5.5 to 5.5
- thermal_anomaly: float32 [256, 32, 4096], P('height', None, 'row'), may hold values from -4 to 4
- foliage_group_index: int32 [256, 32, 4096], P('height', None, 'row'), may hold values from 0 to 7
- paved_surface_flag: int32 [32, 4096], P(None, 'row'), may hold values 0 or 1
- sunlight_flux_crown: float32 [32, 4096], P(None, 'row'), may hold values from 4 to 32
- foliage_area_lookup: float32 [8], replicated, may hold values from 0.02 to 0.2
Outputs:
- u_next: float32 [256, 32, 4096], P('height', None, 'row')
- w_next: float32 [256, 32, 4096], P('height', None, 'row')
- renewed_thermal_anomaly: float32 [256, 32, 4096], P('height', None, 'row')
All inputs are finite; a program needn't handle non-finite values. No bound on the sum of `paved_surface_flag` on one device may be relied on, other than what follows from the above.
Results may differ from a plain program's by a relative error of at most 0.0003.
Values sent between devices are 32-bit elements; how exact they have to be, the bound alone decides.
A program may use at most 64 MiB of HBM per device.

v0:
```python
import math

import jax
import jax.numpy as jnp
from jax import lax
from jax.sharding import PartitionSpec as P

CANOPY = 48


TIME_INCREMENT = 0.25
VISCOSITY = 0.05
DRAG_COEF = 0.2
THERMAL_LIFT = 0.2
SPAN_VAR = 0.25
HAZE_EXTINCT = 0.02
COLUMN_HEIGHT = 256.0
PAVED_ABSORB = 0.9
GRASS_ABSORB = 0.5
HIGHEST_PREC = lax.Precision.HIGHEST


def with_halo(block, sides, width):
    for axis, dim in sides:
        count = lax.axis_size(axis)
        forward = [(i, i + 1) for i in range(count - 1)]
        forward.append((count - 1, 0))
        backward = [(target, source) for source, target in forward]
        low = lax.ppermute(
            lax.slice_in_dim(block, block.shape[dim] - width, None, axis=dim), axis, forward
        )
        high = lax.ppermute(lax.slice_in_dim(block, 0, width, axis=dim), axis, backward)
        block = jnp.concatenate([low, block, high], axis=dim)
    return block


def carried_in(part, axis, combine, identity):
    count = lax.axis_size(axis)
    place = lax.axis_index(axis)
    ahead = count - 1 - place
    gathered = lax.all_gather(part, axis)
    state = jnp.zeros_like(part) + jnp.asarray(identity, part.dtype)

    def one(turn, state):
        source = count - 1 - turn
        return combine(state, lax.dynamic_index_in_dim(gathered, source, 0, False))

    return lax.fori_loop(0, ahead, one, state)


def trig_table(period, first_index, second_index):
    phase_index = first_index[:, None] * second_index[None, :] % period
    angles = phase_index.astype(jnp.float32) * (2.0 * math.pi / period)
    return (jnp.cos(angles), jnp.sin(angles))


def line_tables(length_x):
    inner_len = min(128, length_x)
    outer_len = length_x // inner_len
    slow_index = jnp.arange(outer_len, dtype=jnp.int32)
    fast_index = jnp.arange(inner_len, dtype=jnp.int32)
    return (
        trig_table(outer_len, slow_index, slow_index),
        trig_table(length_x, slow_index, fast_index),
        trig_table(inner_len, fast_index, fast_index),
    )


def hartley_lines(samples, tables, inverse):
    (cos_slow, sin_slow), (cos_turn, sin_turn), (cos_fast, sin_fast) = tables
    outer_len = cos_slow.shape[0]
    inner_len = cos_fast.shape[0]
    lattice = samples.reshape(samples.shape[:-1] + (outer_len, inner_len))
    if inverse:
        real_part = jnp.einsum("...bc,cn->...bn", lattice, cos_fast, precision=HIGHEST_PREC)
        imag_part = -jnp.einsum("...bc,cn->...bn", lattice, sin_fast, precision=HIGHEST_PREC)
    else:
        real_part = jnp.einsum("...an,ab->...bn", lattice, cos_slow, precision=HIGHEST_PREC)
        imag_part = -jnp.einsum("...an,ab->...bn", lattice, sin_slow, precision=HIGHEST_PREC)
    turned_re = real_part * cos_turn + imag_part * sin_turn
    turned_im = imag_part * cos_turn - real_part * sin_turn
    if inverse:
        out_re = jnp.einsum(
            "...bn,ba->...an", turned_re, cos_slow, precision=HIGHEST_PREC
        ) + jnp.einsum("...bn,ba->...an", turned_im, sin_slow, precision=HIGHEST_PREC)
        out_im = jnp.einsum(
            "...bn,ba->...an", turned_im, cos_slow, precision=HIGHEST_PREC
        ) - jnp.einsum("...bn,ba->...an", turned_re, sin_slow, precision=HIGHEST_PREC)
    else:
        out_re = jnp.einsum(
            "...bn,nc->...bc", turned_re, cos_fast, precision=HIGHEST_PREC
        ) + jnp.einsum("...bn,nc->...bc", turned_im, sin_fast, precision=HIGHEST_PREC)
        out_im = jnp.einsum(
            "...bn,nc->...bc", turned_im, cos_fast, precision=HIGHEST_PREC
        ) - jnp.einsum("...bn,nc->...bc", turned_re, sin_fast, precision=HIGHEST_PREC)
    return (out_re - out_im).reshape(samples.shape)


def cosine_levels(count_levels):
    mode_index = jnp.arange(count_levels, dtype=jnp.int32)
    phase_index = mode_index[:, None] * (2 * mode_index[None, :] + 1) % (4 * count_levels)
    angles = phase_index.astype(jnp.float32) * (math.pi / (2.0 * count_levels))
    weights = jnp.where(
        mode_index == 0, math.sqrt(1.0 / count_levels), math.sqrt(2.0 / count_levels)
    ).astype(jnp.float32)
    return jnp.cos(angles) * weights[:, None]


def solve_modes(source_modes, cosine_table, first_freq, length_x):
    count_levels = cosine_table.shape[0]
    freq_count = source_modes.shape[-1]
    inner_len = min(128, length_x)
    freq_index = first_freq + jnp.arange(freq_count, dtype=jnp.int32)
    wavenumber = freq_index // inner_len + length_x // inner_len * (freq_index % inner_len)
    mode_index = jnp.arange(count_levels, dtype=jnp.int32)
    eigen_x = -4.0 * jnp.sin(wavenumber.astype(jnp.float32) * (math.pi / length_x)) ** 2
    eigen_z = -4.0 * jnp.sin(mode_index.astype(jnp.float32) * (math.pi / (2.0 * count_levels))) ** 2
    modal_field = jnp.einsum("mz,zyf->myf", cosine_table, source_modes, precision=HIGHEST_PREC)
    total_eigen = eigen_z[:, None, None] + eigen_x[None, None, :]
    singular = (mode_index[:, None, None] == 0) & (wavenumber[None, None, :] == 0)
    modal_field = jnp.where(singular, 0.0, modal_field / jnp.where(singular, 1.0, total_eigen))
    return jnp.einsum("mz,myf->zyf", cosine_table, modal_field, precision=HIGHEST_PREC)


def add_depths(earlier_sum, later_sum):
    return earlier_sum + later_sum


def per_device(
    streamwise_wind_edges,
    climbing_wind_edges,
    thermal_anomaly,
    foliage_group_index,
    paved_surface_flag,
    sunlight_flux_crown,
    foliage_area_lookup,
):
    level_values = streamwise_wind_edges.shape[0]
    length_z = level_values * lax.axis_size("height")
    length_x = streamwise_wind_edges.shape[2] * lax.axis_size("row")
    height_rank = lax.axis_index("height")
    level_index = height_rank * level_values + jnp.arange(level_values, dtype=jnp.int32)
    top_level = (level_index == length_z - 1)[:, None, None]
    bottom_level = (level_index == 0)[:, None, None]
    joined_arrays = jnp.stack([streamwise_wind_edges, climbing_wind_edges, thermal_anomaly])
    padded = with_halo(joined_arrays, (("row", 3), ("height", 1)), 1)
    leaf_area = jnp.zeros(foliage_group_index.shape, jnp.float32)
    for class_index in range(foliage_area_lookup.shape[0]):
        leaf_area = leaf_area + jnp.where(
            foliage_group_index == class_index, foliage_area_lookup[class_index], 0.0
        )
    leaf_area = jnp.where((level_index < CANOPY)[:, None, None], leaf_area, 0.0)
    thickness = COLUMN_HEIGHT / length_z
    haze = HAZE_EXTINCT * jnp.exp(-4.0 * (level_index.astype(jnp.float32) + 0.5) / length_z)
    optical = (0.5 * leaf_area + haze[:, None, None]) * thickness
    own_depth = jnp.sum(optical, axis=0)
    depth_above = carried_in(own_depth, "height", add_depths, jnp.zeros_like(own_depth))
    inclusive = jnp.flip(jnp.cumsum(jnp.flip(optical, 0), 0), 0)
    depth_top = depth_above[None] + jnp.concatenate(
        [inclusive[1:], jnp.zeros_like(inclusive[:1])], 0
    )
    trans_top = jnp.exp(-depth_top)
    trans_bottom = jnp.exp(-(depth_top + optical))
    sunlight_warming = sunlight_flux_crown[None] * (trans_top - trans_bottom) / thickness
    absorb = jnp.where(paved_surface_flag == 1, PAVED_ABSORB, GRASS_ABSORB)
    surface = jnp.where(
        height_rank == 0, sunlight_flux_crown * trans_bottom[0] * absorb / thickness, 0.0
    )
    sunlight_warming = jnp.concatenate(
        [sunlight_warming[:1] + surface[None], sunlight_warming[1:]], 0
    )
    east_cells = padded[:, 1:-1, :, 2:]
    west_cells = padded[:, 1:-1, :, :-2]
    above_cells = jnp.where(top_level[None], 0.0, padded[:, 2:, :, 1:-1])
    below_cells = jnp.where(bottom_level[None], 0.0, padded[:, :-2, :, 1:-1])
    advect = (
        streamwise_wind_edges[None] * (east_cells - west_cells) * 0.5
        + climbing_wind_edges[None] * (above_cells - below_cells) * 0.5
    )
    diffuse = VISCOSITY * (
        east_cells + west_cells + above_cells + below_cells - 4.0 * joined_arrays
    )
    increment_bundle = diffuse - advect
    wind_speed = jnp.sqrt(
        streamwise_wind_edges * streamwise_wind_edges
        + climbing_wind_edges * climbing_wind_edges
        + SPAN_VAR
    )
    foliage_friction_coefficient = DRAG_COEF * leaf_area * wind_speed
    trial_streamwise_wind = streamwise_wind_edges + TIME_INCREMENT * (
        increment_bundle[0] - foliage_friction_coefficient * streamwise_wind_edges
    )
    trial_climbing_wind = climbing_wind_edges + TIME_INCREMENT * (
        increment_bundle[1]
        - foliage_friction_coefficient * climbing_wind_edges
        + THERMAL_LIFT * thermal_anomaly
    )
    trial_climbing_wind = jnp.where(top_level, 0.0, trial_climbing_wind)
    renewed_thermal_anomaly = thermal_anomaly + TIME_INCREMENT * (
        increment_bundle[2] + sunlight_warming
    )
    tables = line_tables(length_x)
    cosine_table = cosine_levels(length_z)
    freq_share = length_x // lax.axis_size("height")
    first_freq = height_rank * freq_share
    along_wind = lax.all_to_all(
        trial_streamwise_wind, "row", split_axis=1, concat_axis=2, tiled=True
    )
    upward = lax.all_to_all(trial_climbing_wind, "row", split_axis=1, concat_axis=2, tiled=True)
    spread = along_wind - jnp.roll(along_wind, 1, axis=-1)
    both_lines = hartley_lines(jnp.stack([spread, upward]), tables, False)
    spread_lines = both_lines[0]
    upward_lines = both_lines[1]
    spread_modes = lax.all_to_all(spread_lines, "height", split_axis=2, concat_axis=0, tiled=True)
    upward_modes = lax.all_to_all(upward_lines, "height", split_axis=2, concat_axis=0, tiled=True)
    lower_modes = jnp.concatenate([jnp.zeros_like(upward_modes[:1]), upward_modes[:-1]], 0)
    potential = solve_modes(
        spread_modes + (upward_modes - lower_modes), cosine_table, first_freq, length_x
    )
    rise_modes = jnp.concatenate([potential[1:] - potential[:-1], jnp.zeros_like(potential[:1])], 0)
    potential, rise_modes = (potential, rise_modes)
    potential_lines, rise_lines = (
        lax.all_to_all(potential, "height", split_axis=0, concat_axis=2, tiled=True),
        lax.all_to_all(rise_modes, "height", split_axis=0, concat_axis=2, tiled=True),
    )
    restored = hartley_lines(jnp.stack([potential_lines, rise_lines]), tables, True) * (
        1.0 / length_x
    )
    slope_lines = jnp.roll(restored[0], -1, axis=-1) - restored[0]
    streamwise_push_gradient, climbing_push_gradient = (
        lax.all_to_all(slope_lines, "row", split_axis=2, concat_axis=1, tiled=True),
        lax.all_to_all(restored[1], "row", split_axis=2, concat_axis=1, tiled=True),
    )
    return (
        trial_streamwise_wind - streamwise_push_gradient,
        trial_climbing_wind - climbing_push_gradient,
        renewed_thermal_anomaly,
    )


def solution(mesh):
    placed = (
        P("height", None, "row"),
        P("height", None, "row"),
        P("height", None, "row"),
        P("height", None, "row"),
        P(None, "row"),
        P(None, "row"),
        P(),
    )
    return jax.shard_map(
        per_device,
        mesh=mesh,
        in_specs=placed,
        out_specs=(P("height", None, "row"), P("height", None, "row"), P("height", None, "row")),
        check_vma=False,
    )
```

profile of v0, /device:TPU:1, one launch (start us, length us, event | category | flops | bytes accessed | tf_op | source)
XLA Modules:
  0.0 294.8 jit_solution(11993718765217699921)
XLA Ops:
  2.5 13.7 %collective-permute-start = (f32[3,16,32,1]{2,1,3,0:T(8,128)S(1)}, f32[3,16,32,1]{2,1,3,0:T(8,128)S(1)}, u32[]{:S(2)}, u32[]{:S(2)}) collective-permute-start(f32[3,16,32,1]{2,1,3,0:T(8,128)S(1)} %copy.143), channel_id=1, source_target_pairs={{16,0},{32,16},{48,32},{64,48},{80,64},{96,80},{112,96},{128,112},... | collective-permute-start | bytes 18440 | tf_op jit(solution)/shard_map/ppermute | solution.py:32
  19.2 5.2 %fusion.164 = (f32[32,128]{1,0:T(8,128)S(1)}, f32[16,32,128]{2,1,0:T(8,128)S(1)}) fusion(f32[16]{0:T(128)S(1)} %exponential_multiply_fusion, f32[]{:T(128)} %bitcast.12, s32[16,32,128]{2,1,0:T(8,128)S(1)} %copy-done.3, f32[]{:T(128)} %bitcast.11, f32[]{:T(128)} %bitcast.10, f32[]{:T(128)} %bitcast.9, f32[]{:T(128)} %bitcast.8, f32[]{:T(128)} %bitcast.7, ...), kind=kLoop, calls=%fused_computation.234 | loop fusion | flops 1765376 | bytes 540784 | tf_op jit(solution)/shard_map/reduce_sum | solution.py:156
  24.4 19.1 %all-gather = f32[512,128]{1,0:T(8,128)S(1)} all-gather(f32[32,128]{1,0:T(8,128)S(1)} %get-tuple-element.68), channel_id=2, replica_groups=mesh['row'=32,'height'=16] {'height'}, dimensions={0}, use_global_device_ids=true | all-gather | bytes 278528 | tf_op jit(solution)/shard_map/all_gather | solution.py:41
  47.8 2.6 collective-permute-done.2
  52.1 6.2 %fusion.33 = (f32[16,32,128]{2,1,0:T(8,128)S(1)}, f32[16,32,128]{2,1,0:T(8,128)S(1)}, f32[16,32,128]{2,1,0:T(8,128)}) fusion(f32[16,32,128]{2,1,0:T(8,128)S(1)} %copy-done, f32[3,16,32,128]{3,2,1,0:T(8,128)S(1)} %multiply_subtract_fusion, f32[16,32,128]{2,1,0:T(8,128)S(1)} %copy-done.2, f32[16,32,128]{2,1,0:T(8,128)S(1)} %copy-done.1, ...), kind=kLoop, calls=%fused_computation.74 | loop fusion | flops 2949120 | bytes 2883648 | tf_op jit(solution)/shard_map/jit(_where)/select_n | solution.py:198
  59.2 6.7 %all-to-all-start = ((f32[16,32,128]{2,0,1:T(8,128)}), f32[16,32,128]{2,0,1:T(8,128)S(1)}, u32[]{:S(2)}, u32[]{:S(2)}) async-start(f32[16,32,128]{2,0,1:T(8,128)} %copy.149), calls=%async_computation | async-start | bytes 524288 | tf_op jit(solution)/shard_map/all_to_all | solution.py:206
  66.8 8.7 %all-to-all-done = f32[16,32,128]{2,0,1:T(8,128)S(1)} async-done(((f32[16,32,128]{2,0,1:T(8,128)}), f32[16,32,128]{2,0,1:T(8,128)S(1)}, u32[]{:S(2)}, u32[]{:S(2)}) %all-to-all-start) | async-done | bytes 262176 | tf_op jit(solution)/shard_map/all_to_all | solution.py:206
  75.5 6.4 %all-to-all-start.1 = ((f32[16,32,128]{2,0,1:T(8,128)}), f32[16,32,128]{2,0,1:T(8,128)S(1)}, u32[]{:S(2)}, u32[]{:S(2)}) async-start(f32[16,32,128]{2,0,1:T(8,128)} %copy.153), calls=%async_computation.1 | async-start | bytes 524288 | tf_op jit(solution)/shard_map/all_to_all | solution.py:209
  82.5 9.1 %all-to-all-done.1 = f32[16,32,128]{2,0,1:T(8,128)S(1)} async-done(((f32[16,32,128]{2,0,1:T(8,128)}), f32[16,32,128]{2,0,1:T(8,128)S(1)}, u32[]{:S(2)}, u32[]{:S(2)}) %all-to-all-start.1) | async-done | bytes 262176 | tf_op jit(solution)/shard_map/all_to_all | solution.py:209
  97.5 19.3 %reduce.2 = f32[4096,16]{1,0:T(8,128)} reduce(f32[4096,1,16]{2,1,0:T(1,128)S(1)} %bitcast.202, f32[]{:T(128)} %broadcast.432), dimensions={1}, to_apply=%bitcast.184.reduce_sub_computation | reduce | bytes 524292
  116.9 3.0 %reshape.337 = f32[16,1,4096]{2,1,0:T(1,128)} reshape(f32[4096,16]{1,0:T(8,128)} %reduce.2) | data formatting | bytes 524288
  119.9 8.6 %all-to-all-start.3 = ((f32[16,1,4096]{2,1,0:T(1,128)}), f32[16,1,4096]{2,1,0:T(1,128)S(1)}, u32[]{:S(2)}, u32[]{:S(2)}) async-start(f32[16,1,4096]{2,1,0:T(1,128)} %reshape.337), calls=%async_computation.3 | async-start | bytes 524288 | tf_op jit(solution)/shard_map/all_to_all | solution.py:215
  129.1 19.4 %reduce = f32[4096,16]{1,0:T(8,128)} reduce(f32[4096,1,16]{2,1,0:T(1,128)S(1)} %bitcast.203, f32[]{:T(128)} %broadcast.432), dimensions={1}, to_apply=%bitcast.182.reduce_sub_computation | reduce | bytes 524292
  148.5 3.0 %reshape.335 = f32[16,1,4096]{2,1,0:T(1,128)} reshape(f32[4096,16]{1,0:T(8,128)} %reduce) | data formatting | bytes 524288
  151.5 7.2 %all-to-all-start.2 = ((f32[16,1,4096]{2,1,0:T(1,128)}), f32[16,1,4096]{2,1,0:T(1,128)S(1)}, u32[]{:S(2)}, u32[]{:S(2)}) async-start(f32[16,1,4096]{2,1,0:T(1,128)} %reshape.335), calls=%async_computation.2 | async-start | bytes 524288 | tf_op jit(solution)/shard_map/all_to_all | solution.py:214
  160.0 3.9 %reshape.338 = f32[4096,1,16]{2,1,0:T(1,128)S(1)} reshape(f32[16,4096]{1,0:T(8,128)S(1)} %reduce.3) | data formatting | bytes 524288
  164.8 5.6 %all-to-all-done.2 = f32[16,1,4096]{2,1,0:T(1,128)S(1)} async-done(((f32[16,1,4096]{2,1,0:T(1,128)}), f32[16,1,4096]{2,1,0:T(1,128)S(1)}, u32[]{:S(2)}, u32[]{:S(2)}) %all-to-all-start.2) | async-done | bytes 262176 | tf_op jit(solution)/shard_map/all_to_all | solution.py:214
  171.6 3.9 %reshape.336 = f32[4096,1,16]{2,1,0:T(1,128)S(1)} reshape(f32[16,4096]{1,0:T(8,128)S(1)} %reduce.1) | data formatting | bytes 524288
  180.5 3.4 %all-to-all-start.5 = ((f32[256,1,256]{2,1,0:T(1,128)}), f32[256,1,256]{2,1,0:T(1,128)S(1)}, u32[]{:S(2)}, u32[]{:S(2)}) async-start(f32[256,1,256]{2,1,0:T(1,128)} %concatenate.66.clone), calls=%async_computation.5 | async-start | bytes 524288 | tf_op jit(solution)/shard_map/all_to_all | solution.py:224
  185.0 10.2 %all-to-all-done.5 = f32[256,1,256]{2,1,0:T(1,128)S(1)} async-done(((f32[256,1,256]{2,1,0:T(1,128)}), f32[256,1,256]{2,1,0:T(1,128)S(1)}, u32[]{:S(2)}, u32[]{:S(2)}) %all-to-all-start.5) | async-done | bytes 262176 | tf_op jit(solution)/shard_map/all_to_all | solution.py:224
  195.1 3.6 %all-to-all-start.4 = ((f32[256,1,256]{2,1,0:T(1,128)}), f32[256,1,256]{2,1,0:T(1,128)S(1)}, u32[]{:S(2)}, u32[]{:S(2)}) async-start(f32[256,1,256]{2,1,0:T(1,128)} %copy.161), calls=%async_computation.4 | async-start | bytes 524288 | tf_op jit(solution)/shard_map/all_to_all | solution.py:223
  198.9 11.5 %all-to-all-done.4 = f32[256,1,256]{2,1,0:T(1,128)S(1)} async-done(((f32[256,1,256]{2,1,0:T(1,128)}), f32[256,1,256]{2,1,0:T(1,128)S(1)}, u32[]{:S(2)}, u32[]{:S(2)}) %all-to-all-start.4) | async-done | bytes 262176 | tf_op jit(solution)/shard_map/all_to_all | solution.py:223
  215.8 19.4 %reduce.6 = f32[4096,16]{1,0:T(8,128)} reduce(f32[4096,1,16]{2,1,0:T(1,128)S(1)} %bitcast.204, f32[]{:T(128)} %broadcast.432), dimensions={1}, to_apply=%bitcast.188.reduce_sub_computation | reduce | bytes 524292
  235.2 3.0 %reshape.341 = f32[32,1,2048]{2,1,0:T(1,128)} reshape(f32[4096,16]{1,0:T(8,128)} %reduce.6) | data formatting | bytes 524288
  238.2 4.8 %all-to-all-start.7 = ((f32[32,1,2048]{2,1,0:T(1,128)}), f32[32,1,2048]{2,1,0:T(1,128)}, u32[]{:S(2)}, u32[]{:S(2)}) async-start(f32[32,1,2048]{2,1,0:T(1,128)} %reshape.341), calls=%async_computation.7 | async-start | bytes 524288 | tf_op jit(solution)/shard_map/all_to_all | solution.py:232
  243.1 2.4 copy.165
  245.5 19.3 %reduce.4 = f32[4096,16]{1,0:T(8,128)} reduce(f32[4096,1,16]{2,1,0:T(1,128)S(1)} %bitcast.205, f32[]{:T(128)} %broadcast.432), dimensions={1}, to_apply=%bitcast.186.reduce_sub_computation | reduce | bytes 524292
  264.9 3.0 %reshape.339 = f32[32,1,2048]{2,1,0:T(1,128)} reshape(f32[4096,16]{1,0:T(8,128)} %reduce.4) | data formatting | bytes 524288
  267.9 9.6 %all-to-all-start.6 = ((f32[32,1,2048]{2,1,0:T(1,128)}), f32[32,1,2048]{2,1,0:T(1,128)S(1)}, u32[]{:S(2)}, u32[]{:S(2)}) async-start(f32[32,1,2048]{2,1,0:T(1,128)} %reshape.339), calls=%async_computation.6 | async-start | bytes 524288 | tf_op jit(solution)/shard_map/all_to_all | solution.py:231
  279.7 3.9 %reshape.342 = f32[4096,1,16]{2,1,0:T(1,128)S(1)} reshape(f32[32,2048]{1,0:T(8,128)S(1)} %reduce.7) | data formatting | bytes 524288
  285.0 2.9 all-to-all-done.6
  289.2 3.9 %reshape.340 = f32[4096,1,16]{2,1,0:T(1,128)S(1)} reshape(f32[32,2048]{1,0:T(8,128)S(1)} %reduce.5) | data formatting | bytes 524288
  (119 shorter events, 40.6 us)
Async XLA Ops:
  1.8 16.7 %copy-start.5 = (f32[8]{0:T(128)S(1)}, f32[8]{0:T(128)}, u32[]{:S(2)}) copy-start(f32[8]{0:T(128)} %param.15) | copy-start | bytes 100
  1.8 17.4 %copy-start.3 = (s32[16,32,128]{2,1,0:T(8,128)S(1)}, s32[16,32,128]{2,1,0:T(8,128)}, u32[]{:S(2)}) copy-start(s32[16,32,128]{2,1,0:T(8,128)} %param.12) | copy-start | bytes 786436
  2.5 42.6 %collective-permute-start = (f32[3,16,32,1]{2,1,3,0:T(8,128)S(1)}, f32[3,16,32,1]{2,1,3,0:T(8,128)S(1)}, u32[]{:S(2)}, u32[]{:S(2)}) collective-permute-start(f32[3,16,32,1]{2,1,3,0:T(8,128)S(1)} %copy.143), channel_id=1, source_target_pairs={{16,0},{32,16},{48,32},{64,48},{80,64},{96,80},{112,96},{128,112},... | collective-permute-start | bytes 18440 | tf_op jit(solution)/shard_map/ppermute | solution.py:32
  16.2 28.8 %copy-start.4 = (f32[32,128]{1,0:T(8,128)S(1)}, f32[32,128]{1,0:T(8,128)}, u32[]{:S(2)}) copy-start(f32[32,128]{1,0:T(8,128)} %param.14) | copy-start | bytes 49156
  16.5 28.9 %collective-permute-start.1 = (f32[3,16,32,1]{2,1,3,0:T(8,128)S(1)}, f32[3,16,32,1]{2,1,3,0:T(8,128)S(1)}, u32[]{:S(2)}, u32[]{:S(2)}) collective-permute-start(f32[3,16,32,1]{2,1,3,0:T(8,128)S(1)} %copy.145), channel_id=1, source_target_pairs={{0,16},{16,32},{32,48},{48,64},{64,80},{80,96},{96,112},{112,128},... | collective-permute-start | bytes 18440 | tf_op jit(solution)/shard_map/ppermute | solution.py:29
  19.2 25.8 %copy-start.6 = (s32[32,128]{1,0:T(8,128)S(1)}, s32[32,128]{1,0:T(8,128)}, u32[]{:S(2)}) copy-start(s32[32,128]{1,0:T(8,128)} %param.13) | copy-start | bytes 49156
  44.1 1.7 copy-start
  44.1 1.7 copy-start.1
  44.1 1.7 copy-start.2
  46.0 4.3 %collective-permute-start.2 = (f32[3,1,32,130]{3,2,1,0:T(8,128)S(1)}, f32[3,1,32,130]{3,2,1,0:T(8,128)S(1)}, u32[]{:S(2)}, u32[]{:S(2)}) collective-permute-start(f32[3,1,32,130]{3,2,1,0:T(8,128)S(1)} %get-tuple-element.70), channel_id=1, source_target_pairs={{1,0},{2,1},{3,2},{4,3},{5,4},{6,5},{7,6},{8,7},{9,8},{10,9},{11,1... | collective-permute-start | bytes 149768 | tf_op jit(solution)/shard_map/ppermute | solution.py:32
  46.2 4.2 %collective-permute-start.3 = (f32[3,1,32,130]{3,2,1,0:T(8,128)S(1)}, f32[3,1,32,130]{3,2,1,0:T(8,128)S(1)}, u32[]{:S(2)}, u32[]{:S(2)}) collective-permute-start(f32[3,1,32,130]{3,2,1,0:T(8,128)S(1)} %get-tuple-element.71), channel_id=1, source_target_pairs={{0,1},{1,2},{2,3},{3,4},{4,5},{5,6},{6,7},{7,8},{8,9},{9,10},{10,1... | collective-permute-start | bytes 149768 | tf_op jit(solution)/shard_map/ppermute | solution.py:29
  59.2 16.4 %all-to-all-start = ((f32[16,32,128]{2,0,1:T(8,128)}), f32[16,32,128]{2,0,1:T(8,128)S(1)}, u32[]{:S(2)}, u32[]{:S(2)}) async-start(f32[16,32,128]{2,0,1:T(8,128)} %copy.149), calls=%async_computation | async-start | bytes 524288 | tf_op jit(solution)/shard_map/all_to_all | solution.py:206
  75.5 16.1 %all-to-all-start.1 = ((f32[16,32,128]{2,0,1:T(8,128)}), f32[16,32,128]{2,0,1:T(8,128)S(1)}, u32[]{:S(2)}, u32[]{:S(2)}) async-start(f32[16,32,128]{2,0,1:T(8,128)} %copy.153), calls=%async_computation.1 | async-start | bytes 524288 | tf_op jit(solution)/shard_map/all_to_all | solution.py:209
  119.9 31.6 %all-to-all-start.3 = ((f32[16,1,4096]{2,1,0:T(1,128)}), f32[16,1,4096]{2,1,0:T(1,128)S(1)}, u32[]{:S(2)}, u32[]{:S(2)}) async-start(f32[16,1,4096]{2,1,0:T(1,128)} %reshape.337), calls=%async_computation.3 | async-start | bytes 524288 | tf_op jit(solution)/shard_map/all_to_all | solution.py:215
  151.5 18.9 %all-to-all-start.2 = ((f32[16,1,4096]{2,1,0:T(1,128)}), f32[16,1,4096]{2,1,0:T(1,128)S(1)}, u32[]{:S(2)}, u32[]{:S(2)}) async-start(f32[16,1,4096]{2,1,0:T(1,128)} %reshape.335), calls=%async_computation.2 | async-start | bytes 524288 | tf_op jit(solution)/shard_map/all_to_all | solution.py:214
  180.5 14.6 %all-to-all-start.5 = ((f32[256,1,256]{2,1,0:T(1,128)}), f32[256,1,256]{2,1,0:T(1,128)S(1)}, u32[]{:S(2)}, u32[]{:S(2)}) async-start(f32[256,1,256]{2,1,0:T(1,128)} %concatenate.66.clone), calls=%async_computation.5 | async-start | bytes 524288 | tf_op jit(solution)/shard_map/all_to_all | solution.py:224
  195.1 15.3 %all-to-all-start.4 = ((f32[256,1,256]{2,1,0:T(1,128)}), f32[256,1,256]{2,1,0:T(1,128)S(1)}, u32[]{:S(2)}, u32[]{:S(2)}) async-start(f32[256,1,256]{2,1,0:T(1,128)} %copy.161), calls=%async_computation.4 | async-start | bytes 524288 | tf_op jit(solution)/shard_map/all_to_all | solution.py:223
  238.2 29.7 %all-to-all-start.7 = ((f32[32,1,2048]{2,1,0:T(1,128)}), f32[32,1,2048]{2,1,0:T(1,128)}, u32[]{:S(2)}, u32[]{:S(2)}) async-start(f32[32,1,2048]{2,1,0:T(1,128)} %reshape.341), calls=%async_computation.7 | async-start | bytes 524288 | tf_op jit(solution)/shard_map/all_to_all | solution.py:232
  267.9 20.0 %all-to-all-start.6 = ((f32[32,1,2048]{2,1,0:T(1,128)}), f32[32,1,2048]{2,1,0:T(1,128)S(1)}, u32[]{:S(2)}, u32[]{:S(2)}) async-start(f32[32,1,2048]{2,1,0:T(1,128)} %reshape.339), calls=%async_computation.6 | async-start | bytes 524288 | tf_op jit(solution)/shard_map/all_to_all | solution.py:231
where the time goes:
time: 301 us; the launch traced here: 295 us
  other arithmetic  101 us (34%)
  starting transfers between devices  67.7 us (22%)
  waiting for transfers between devices  50.5 us (17%)
  local copies, waits for them, and re-layouts  42.7 us (14%)
  blocking collectives  19.1 us (6%)
  matrix products  11.8 us (4%)
    unnamed x5, other arithmetic  77.5 us
    unnamed x25, local copies, waits for them, and re-layouts  28.7 us
    all_gather x1, blocking collectives, carried_in(): gathered = lax.all_gather(part, axis)  19.1 us
    ppermute x2, starting transfers between devices, with_halo(): lax.ppermute(lax.slice_in_dim(block, 0, width, axis=dim), axis, backward)  13.9 us
    all_to_all x1, waiting for transfers between devices, per_device(): lax.all_to_all(potential, 'height', split_axis=0, concat_axis=2, tiled=True)  11.5 us
    all_to_all x1, waiting for transfers between devices, per_device(): lax.all_to_all(rise_modes, 'height', split_axis=0, concat_axis=2, tiled=T...  10.2 us
    all_to_all x1, starting transfers between devices, per_device(): lax.all_to_all(slope_lines, 'row', split_axis=2, concat_axis=1, tiled=True)  9.59 us
    all_to_all x1, waiting for transfers between devices, per_device(): lax.all_to_all(trial_climbing_wind, 'row', split_axis=1, concat_axis=2, t...  9.1 us
  transfers between devices with their start and end apart: 12, of which 7 were waited for; matrix products, arithmetic and copies ran while one was open for 24% of the time, Pallas kernels for 0%

commit v1 on v0

v1 whole, which is shorter than its diff:
```python
import functools
import math

import jax
import jax.numpy as jnp
import numpy as np
from jax import lax
from jax.experimental import pallas as pl
from jax.experimental.pallas import tpu as pltpu
from jax.sharding import PartitionSpec as P

CANOPY = 48
DT = 0.25
VISCOSITY = 0.05
DRAG_COEF = 0.2
THERMAL_LIFT = 0.2
SPAN_VAR = 0.25
HAZE_EXTINCT = 0.02
PAVED_ABSORB = 0.9
GRASS_ABSORB = 0.5
MESH = pl.DeviceIdType.MESH
HIGHEST = lax.Precision.HIGHEST
LANES = 128


def tables(levels, columns, row_count):
    m = np.arange(levels, dtype=np.float64)
    z = np.arange(levels, dtype=np.float64)
    cosine = np.cos(np.pi * m[:, None] * (z[None, :] + 0.5) / levels)
    cosine *= np.where(m == 0, math.sqrt(1.0 / levels), math.sqrt(2.0 / levels))[:, None]
    mu = 2.0 * np.arcsinh(np.sin(np.pi * m / (2.0 * levels)))
    safe = np.where(m == 0, 1.0, mu)
    gain = np.where(m == 0, 0.0, -1.0 / (2.0 * np.sinh(safe)))
    x = np.arange(LANES, dtype=np.float64)
    rates = np.zeros((levels, LANES))
    for k in range(7):
        rates[:, k] = np.exp(-mu * 2.0**k)
    rates[:, 7] = gain
    phi_west = np.where(m[:, None] == 0, 1.0, gain[:, None] * np.exp(-mu[:, None] * (x + 1.0)))
    phi_east = np.where(m[:, None] == 0, x, gain[:, None] * np.exp(-mu[:, None] * (LANES - x)))
    near = 0.5 * np.abs(x[:, None] - x[None, :]) + x[:, None] * x[None, :] / columns
    lane = np.arange(LANES)
    odd = lane % 2 == 1
    group = np.where(odd, (lane + 1) // 2, lane // 2) % 64
    per_plane = levels // 8
    used = group < 2 * per_plane
    mode = 8 * (group % per_plane)[None, :] + np.arange(8)[:, None]
    mode_mu = mu[mode]
    safe_mu = np.where(mode == 0, 1.0, mode_mu)
    direct = np.zeros((row_count, 8, LANES))
    cross = np.zeros((row_count, 8, LANES))
    for shift in range(row_count):
        to_east = shift if shift else row_count
        to_west = row_count - shift
        steps = np.where(odd, to_west, to_east)[None, :]
        usual = np.exp(-safe_mu * LANES * (steps - 1)) / (1.0 - np.exp(-safe_mu * columns))
        away = float(LANES * shift)
        if shift:
            zero_direct = np.where(odd, away / 2 - away**2 / (2 * columns), 1.0 / columns)
            zero_cross = np.where(odd, -0.5 + away / columns, 0.5 - away / columns)
        else:
            zero_direct = np.zeros(LANES)
            zero_cross = np.zeros(LANES)
        direct[shift] = np.where(mode == 0, zero_direct[None, :], usual) * used
        cross[shift] = np.where(mode == 0, zero_cross[None, :], 0.0) * used
    haze = HAZE_EXTINCT * np.exp(-4.0 * (z + 0.5) / levels)
    haze_above = np.concatenate([np.cumsum(haze[::-1])[::-1], [0.0]])
    f32 = lambda a: np.ascontiguousarray(a, dtype=np.float32)
    return dict(
        cosine=f32(cosine), cosine_t=f32(cosine.T), rates=f32(rates), phi_west=f32(phi_west),
        phi_east=f32(phi_east), near=f32(near), direct=f32(direct), cross=f32(cross),
        haze=f32(haze_above),
    )


def kernel(
    rows, heights,
    u_hbm, w_hbm, t_hbm, class_ref, paved_ref, sun_ref, lookup_ref, haze_ref,
    cosine_ref, cosine_t_ref, rates_ref, phi_w_ref, phi_e_ref, near_ref, direct_ref, cross_ref,
    un_ref, wn_ref, tn_ref,
    ext, leaf, leaf_sum, leaf_in, side_out, side_in, side, us, ws, us_out, us_in,
    d_out, d_in, pm, mom, p_out, p_in, p_up, pc_out, pc_in,
    in_sem, z_sem, side_sem, leaf_sem, star_sem, a2a_sem, mom_sem, back_sem, edge_sem,
):
    r = lax.axis_index("row")
    h = lax.axis_index("height")
    levels_here = class_ref.shape[0]
    planes = class_ref.shape[1]
    nz = levels_here * heights
    block = 2 * levels_here
    groups = nz // 8

    def at(dr, dh):
        return (lax.rem(r + dr + rows, rows), lax.rem(h + dh + heights, heights))

    loads = [
        pltpu.make_async_copy(ref, ext.at[f, pl.ds(1, levels_here)], in_sem.at[f])
        for f, ref in enumerate((u_hbm, w_hbm, t_hbm))
    ]
    for load in loads:
        load.start()

    barrier = pltpu.get_barrier_semaphore()

    def greet_height(i, c):
        pl.semaphore_signal(barrier, inc=1, device_id=at(0, i), device_id_type=MESH)
        return c

    def greet_row(i, c):
        pl.semaphore_signal(barrier, inc=1, device_id=at(i, 0), device_id_type=MESH)
        return c

    lax.fori_loop(1, heights, greet_height, 0)
    lax.fori_loop(1, rows, greet_row, 0)
    for load in loads:
        load.wait()
    lane = lax.broadcasted_iota(jnp.int32, (planes, LANES), 1)

    def pack_sides(z, acc):
        for f in range(3):
            j = 2 * (f * levels_here + z)
            turned = pltpu.roll(ext[f, z + 1], j, 1)
            mine = (lane == j) | (lane == lax.rem(j + LANES - 1, LANES))
            acc = jnp.where(mine, turned, acc)
        return acc

    side_out[...] = lax.fori_loop(0, levels_here, pack_sides, jnp.zeros((planes, LANES), jnp.float32))
    pl.semaphore_wait(barrier, heights + rows - 2)

    def remote(src, dst, sems, slot, device):
        return pltpu.make_async_remote_copy(
            src_ref=src, dst_ref=dst, send_sem=sems.at[0, slot], recv_sem=sems.at[1, slot],
            device_id=device, device_id_type=MESH,
        )

    halo = [
        remote(side_out, side_in.at[0], side_sem, 0, at(1, 0)),
        remote(side_out, side_in.at[1], side_sem, 1, at(-1, 0)),
        remote(ext.at[:, levels_here], ext.at[:, 0], z_sem, 0, at(0, 1)),
        remote(ext.at[:, 1], ext.at[:, levels_here + 1], z_sem, 1, at(0, -1)),
    ]
    for copy in halo:
        copy.start()

    def leaf_level(z, total):
        classes = class_ref[z]
        area = jnp.zeros((planes, LANES), jnp.float32)
        for c in range(lookup_ref.shape[0]):
            area = jnp.where(classes == c, lookup_ref[c], area)
        area = jnp.where(h * levels_here + z < CANOPY, area, 0.0)
        leaf[z] = area
        return total + area

    leaf_sum[...] = lax.fori_loop(0, levels_here, leaf_level, jnp.zeros((planes, LANES), jnp.float32))
    leaf_copies = [
        remote(leaf_sum, leaf_in.at[0], leaf_sem, 0, at(0, -1)),
        remote(leaf_sum, leaf_in.at[1], leaf_sem, 1, at(0, -2)),
    ]
    for copy in leaf_copies:
        copy.start()

    for copy in halo:
        copy.wait()

    @pl.when(h == 0)
    def _():
        ext[:, 0] = jnp.zeros((3, planes, LANES), jnp.float32)

    @pl.when(h == heights - 1)
    def _():
        ext[:, levels_here + 1] = jnp.zeros((3, planes, LANES), jnp.float32)

    even = lax.rem(lane, 2) == 0
    side[...] = jnp.where(even, pltpu.roll(side_in[0], 1, 1), pltpu.roll(side_in[1], LANES - 1, 1))

    def growth(f, z, u, w):
        q = ext[f, z + 1]
        j = 2 * (f * levels_here + z)
        edge = pltpu.roll(side[...], lax.rem(LANES - j, LANES), 1)
        east = jnp.where(lane == LANES - 1, edge, pltpu.roll(q, LANES - 1, 1))
        west = jnp.where(lane == 0, edge, pltpu.roll(q, 1, 1))
        above = ext[f, z + 2]
        below = ext[f, z]
        advect = u * (east - west) * 0.5 + w * (above - below) * 0.5
        diffuse = VISCOSITY * (east + west + above + below - 4.0 * q)
        return diffuse - advect

    def winds(z, acc):
        u = ext[0, z + 1]
        w = ext[1, z + 1]
        t = ext[2, z + 1]
        friction = DRAG_COEF * leaf[z] * jnp.sqrt(u * u + w * w + SPAN_VAR)
        u_star = u + DT * (growth(0, z, u, w) - friction * u)
        w_star = w + DT * (growth(1, z, u, w) - friction * w + THERMAL_LIFT * t)
        w_star = jnp.where(h * levels_here + z == nz - 1, 0.0, w_star)
        us[z] = u_star
        ws[z + 1] = w_star
        return jnp.where(lane == z, pltpu.roll(u_star, z + 1, 1), acc)

    us_out[...] = lax.fori_loop(0, levels_here, winds, jnp.zeros((planes, LANES), jnp.float32))
    star = [
        remote(us_out, us_in, star_sem, 0, at(1, 0)),
        remote(ws.at[levels_here], ws.at[0], star_sem, 1, at(0, 1)),
    ]
    for copy in star:
        copy.start()
    for copy in star:
        copy.wait()

    @pl.when(h == 0)
    def _():
        ws[0] = jnp.zeros((planes, LANES), jnp.float32)

    def divergence(z, c):
        u_star = us[z]
        edge = pltpu.roll(us_in[...], lax.rem(LANES - z, LANES), 1)
        west = jnp.where(lane == 0, edge, pltpu.roll(u_star, 1, 1))
        d_out[pl.ds(z, planes, stride=levels_here), :] = u_star - west + (ws[z + 1] - ws[z])
        return c

    lax.fori_loop(0, levels_here, divergence, 0)

    def exchange(out, into, sems):
        def send(i, c):
            to = lax.rem(h + i, heights)
            pltpu.make_async_remote_copy(
                src_ref=out.at[pl.ds(to * block, block)], dst_ref=into.at[pl.ds(h * block, block)],
                send_sem=sems.at[0], recv_sem=sems.at[1],
                device_id=(r, to), device_id_type=MESH,
            ).start()
            return c

        lax.fori_loop(1, heights, send, 0)
        mine = pl.ds(h * block, block)
        into[mine] = out[mine]

    def finish(buffer, count, sem):
        part = buffer.at[pl.ds(0, count)]
        pltpu.make_async_copy(part, part, sem).wait()

    exchange(d_out, d_in, a2a_sem)

    for copy in leaf_copies:
        copy.wait()
    above1 = jnp.where(h < heights - 1, leaf_in[0], 0.0)
    above2 = jnp.where(h < heights - 2, leaf_in[1], 0.0)
    over = above1 + above2
    sun = sun_ref[...]
    first = jnp.exp(-(0.5 * over + haze_ref[h * levels_here + levels_here]))

    def heat(k, state):
        over, top = state
        z = levels_here - 1 - k
        over = over + leaf[z]
        bottom = jnp.exp(-(0.5 * over + haze_ref[h * levels_here + z]))
        warming = sun * (top - bottom)
        absorb = jnp.where(paved_ref[...] == 1, PAVED_ABSORB, GRASS_ABSORB)
        warming = warming + jnp.where(h * levels_here + z == 0, sun * bottom * absorb, 0.0)
        t = ext[2, z + 1]
        tn_ref[z] = t + DT * (growth(2, z, ext[0, z + 1], ext[1, z + 1]) + warming)
        return over, bottom

    lax.fori_loop(0, levels_here, heat, (over, first))

    finish(d_in, (heights - 1) * block, a2a_sem.at[1])
    grid = d_in[...].reshape(heights, 2, levels_here, LANES)
    both = jnp.concatenate([grid[:, 0].reshape(nz, LANES), grid[:, 1].reshape(nz, LANES)], axis=1)
    modes = jnp.dot(cosine_ref[...], both, precision=HIGHEST, preferred_element_type=jnp.float32)
    pm[...] = modes

    lane8 = lax.broadcasted_iota(jnp.int32, (8, LANES), 1)
    sub8 = lax.broadcasted_iota(jnp.int32, (8, LANES), 0)

    packed = jnp.zeros((8, LANES), jnp.float32)
    for y in range(2):
        columns = pl.ds(y * LANES, LANES)

        def scan_rows(g, acc, y=y, columns=columns):
            at_rows = pl.ds(pl.multiple_of(g * 8, 8), 8)
            d = pm[at_rows, columns]
            rate = rates_ref[at_rows, :]
            fwd = d
            bwd = d
            for k in range(7):
                s = 1 << k
                rk = jnp.broadcast_to(rate[:, k : k + 1], (8, LANES))
                fwd = fwd + rk * jnp.where(lane8 >= s, pltpu.roll(fwd, s, 1), 0.0)
                bwd = bwd + rk * jnp.where(lane8 < LANES - s, pltpu.roll(bwd, LANES - s, 1), 0.0)
            gain = jnp.broadcast_to(rate[:, 7:8], (8, LANES))
            pm[at_rows, columns] = gain * (fwd + bwd - d)
            j = 2 * (y * groups + g)
            ends = jnp.where(lane8 == 0, bwd, fwd)
            turned = pltpu.roll(ends, j, 1)
            mine = (lane8 == j) | (lane8 == lax.rem(j + LANES - 1, LANES))
            return jnp.where(mine, turned, acc)

        zero = modes[0:8, y * LANES : (y + 1) * LANES]
        packed = lax.fori_loop(0, groups, scan_rows, packed)
        own = jnp.dot(zero, near_ref[...], precision=HIGHEST, preferred_element_type=jnp.float32)
        pm[0:8, columns] = jnp.where(sub8 == 0, own, pm[0:8, columns])
        first_moment = jnp.sum(zero * lane8.astype(jnp.float32), axis=1, keepdims=True)
        slot = (sub8 == 0) & (lane8 == 2 * y * groups)
        packed = jnp.where(slot, jnp.broadcast_to(first_moment, (8, LANES)), packed)

    mom[r] = packed

    def send_moments(i, c):
        pltpu.make_async_remote_copy(
            src_ref=mom.at[r], dst_ref=mom.at[r], send_sem=mom_sem.at[0], recv_sem=mom_sem.at[1],
            device_id=at(i, 0), device_id_type=MESH,
        ).start()
        return c

    lax.fori_loop(1, rows, send_moments, 0)
    finish(mom, rows - 1, mom_sem.at[1])

    def gather_moments(i, state):
        direct, cross = state
        values = mom[lax.rem(r + i, rows)]
        return direct + direct_ref[i] * values, cross + cross_ref[i] * values

    nothing = jnp.zeros((8, LANES), jnp.float32)
    direct, cross = lax.fori_loop(0, rows, gather_moments, (nothing, nothing))
    inflow = direct + jnp.where(
        lax.rem(lane8, 2) == 0, pltpu.roll(cross, 1, 1), pltpu.roll(cross, LANES - 1, 1)
    )

    for y in range(2):
        columns = pl.ds(y * LANES, LANES)

        def add_inflow(g, c, y=y, columns=columns):
            at_rows = pl.ds(pl.multiple_of(g * 8, 8), 8)
            j = 2 * (y * groups + g)
            turned = pltpu.roll(inflow, lax.rem(LANES - j, LANES), 1)
            from_east = jnp.broadcast_to(turned[:, 0:1], (8, LANES))
            from_west = jnp.broadcast_to(turned[:, LANES - 1 : LANES], (8, LANES))
            pm[at_rows, columns] = (
                pm[at_rows, columns]
                + phi_w_ref[at_rows, :] * from_west
                + phi_e_ref[at_rows, :] * from_east
            )
            return c

        lax.fori_loop(0, groups, add_inflow, 0)

    solved = jnp.dot(cosine_t_ref[...], pm[...], precision=HIGHEST, preferred_element_type=jnp.float32)
    halves = [
        solved[:, y * LANES : (y + 1) * LANES].reshape(heights, 1, levels_here, LANES) for y in range(2)
    ]
    p_out[...] = jnp.concatenate(halves, axis=1).reshape(nz * 2, LANES)
    exchange(p_out, p_in, back_sem)
    finish(p_in, (heights - 1) * block, back_sem.at[1])

    def first_columns(z, acc):
        p = p_in[pl.ds(z, planes, stride=levels_here), :]
        return jnp.where(lane == z, pltpu.roll(p, z, 1), acc)

    pc_out[0] = lax.fori_loop(0, levels_here, first_columns, jnp.zeros((planes, LANES), jnp.float32))
    pc_out[1] = p_in[pl.ds(0, planes, stride=levels_here), :]
    edges = [
        remote(pc_out.at[0], pc_in, edge_sem, 0, at(-1, 0)),
        remote(pc_out.at[1], p_up, edge_sem, 1, at(0, -1)),
    ]
    for copy in edges:
        copy.start()
    for copy in edges:
        copy.wait()

    def project(z, p):
        edge = pltpu.roll(pc_in[...], LANES - 1 - z, 1)
        east = jnp.where(lane == LANES - 1, edge, pltpu.roll(p, LANES - 1, 1))
        un_ref[z] = us[z] - (east - p)
        inside = p_in[pl.ds(jnp.minimum(z + 1, levels_here - 1), planes, stride=levels_here), :]
        above = jnp.where(z == levels_here - 1, p_up[...], inside)
        rise = jnp.where(h * levels_here + z == nz - 1, 0.0, above - p)
        wn_ref[z] = ws[z + 1] - rise
        return above

    lax.fori_loop(0, levels_here, project, pc_out[1])

    finish(d_out, (heights - 1) * block, a2a_sem.at[0])
    finish(mom, rows - 1, mom_sem.at[0])
    finish(p_out, (heights - 1) * block, back_sem.at[0])


def solution(mesh):
    rows, heights = mesh.shape["row"], mesh.shape["height"]

    def per_device(u, w, t, classes, paved, sun, lookup):
        levels_here, planes, width = u.shape
        nz = levels_here * heights
        table = tables(nz, width * rows, rows)
        vmem = pl.BlockSpec(memory_space=pltpu.VMEM)
        smem = pl.BlockSpec(memory_space=pltpu.SMEM)
        hbm = pl.BlockSpec(memory_space=pl.ANY)
        field = jax.ShapeDtypeStruct(u.shape, jnp.float32)
        plane = (planes, LANES)
        f32 = jnp.float32
        dma = pltpu.SemaphoreType.DMA
        call = pl.pallas_call(
            functools.partial(kernel, rows, heights),
            out_shape=(field, field, field),
            in_specs=[hbm] * 3 + [vmem] * 3 + [smem] * 2 + [vmem] * 8,
            out_specs=(vmem, vmem, vmem),
            scratch_shapes=[
                pltpu.VMEM((3, levels_here + 2) + plane, f32),
                pltpu.VMEM((levels_here,) + plane, f32),
                pltpu.VMEM(plane, f32),
                pltpu.VMEM((2,) + plane, f32),
                pltpu.VMEM(plane, f32),
                pltpu.VMEM((2,) + plane, f32),
                pltpu.VMEM(plane, f32),
                pltpu.VMEM((levels_here,) + plane, f32),
                pltpu.VMEM((levels_here + 1,) + plane, f32),
                pltpu.VMEM(plane, f32),
                pltpu.VMEM(plane, f32),
                pltpu.VMEM((2 * nz, LANES), f32),
                pltpu.VMEM((2 * nz, LANES), f32),
                pltpu.VMEM((nz, 2 * LANES), f32),
                pltpu.VMEM((rows, 8, LANES), f32),
                pltpu.VMEM((2 * nz, LANES), f32),
                pltpu.VMEM((2 * nz, LANES), f32),
                pltpu.VMEM(plane, f32),
                pltpu.VMEM((2,) + plane, f32),
                pltpu.VMEM(plane, f32),
                dma((3,)), dma((2, 2)), dma((2, 2)), dma((2, 2)), dma((2, 2)),
                dma((2,)), dma((2,)), dma((2,)), dma((2, 2)),
            ],
            compiler_params=pltpu.CompilerParams(
                collective_id=0, has_side_effects=True, vmem_limit_bytes=32 * 1024 * 1024
            ),
        )
        return call(
            u, w, t, classes, paved, sun, lookup, table["haze"], table["cosine"],
            table["cosine_t"], table["rates"], table["phi_west"], table["phi_east"],
            table["near"], table["direct"], table["cross"],
        )

    field = P("height", None, "row")
    line = P(None, "row")
    return jax.shard_map(
        per_device, mesh=mesh, in_specs=(field, field, field, field, line, line, P()),
        out_specs=(field, field, field), check_vma=False,
    )
```

time: 301 us -> 120 us (0.40); the launches traced: 295 us -> 119 us
  Pallas kernels: 0 us -> 103 us
  other arithmetic: 101 us -> 0 us
  starting transfers between devices: 67.7 us -> 0 us
  waiting for transfers between devices: 50.5 us -> 0 us
  local copies, waits for them, and re-layouts: 42.7 us -> 15.9 us
  blocking collectives: 19.1 us -> 0 us
  matrix products: 11.8 us -> 0 us
    pallas_call x0 -> x1, Pallas kernels: none -> 103 us  [per_device(): call(u, w, t, classes, paved, sun, lookup, table['haze'], table['cosine']...]
    unnamed x5 -> x0, other arithmetic: 77.5 us -> none
    all_to_all x8 -> x0, starting transfers between devices: 50.4 us -> none  [the longest x1 9.59 us: per_device(): lax.all_to_all(slope_lines, 'row', split_axis=2, concat_axis=1, tiled=True)]
    all_to_all x8 -> x0, waiting for transfers between devices: 47.9 us -> none  [the longest x1 11.5 us: per_device(): lax.all_to_all(potential, 'height', split_axis=0, concat_axis=2, tiled=True)]
    all_gather x1 -> x0, blocking collectives: 19.1 us -> none  [carried_in(): gathered = lax.all_gather(part, axis)]
    ppermute x4 -> x0, starting transfers between devices: 17.4 us -> none  [the longest x2 13.9 us: with_halo(): lax.ppermute(lax.slice_in_dim(block, 0, width, axis=dim), axis, backward)]
    unnamed x25 -> x35, local copies, waits for them, and re-layouts: 28.7 us -> 15.9 us
    dot_general x14 -> x0, matrix products: 11.8 us -> none  [the longest x1 1.5 us: solve_modes(): jnp.einsum('mz,myf->zyf', cosine_table, modal_field, precision=HIGHEST_PREC)]
  transfers between devices with their start and end apart: 12 -> 0, of which waited for: 7 -> 0; matrix products, arithmetic and copies ran while one was open for 24% -> 0% of each run, Pallas kernels for 0% -> 0%
where the time goes in v1:
time: 120 us; the launch traced here: 119 us
  Pallas kernels  103 us (86%)
  local copies, waits for them, and re-layouts  15.9 us (13%)
    pallas_call x1, Pallas kernels, per_device(): call(u, w, t, classes, paved, sun, lookup, table['haze'], table['cosine']...  103 us
    unnamed x35, local copies, waits for them, and re-layouts  15.9 us

profile of v1, /device:TPU:1, one launch (start us, length us, event | category | flops | bytes accessed | tf_op | source)
XLA Modules:
  0.0 119.1 jit_solution(16890080115157310030)
XLA Ops:
  0.6 0.0 copy-start
  0.6 0.9 copy-done
  1.6 0.0 copy-start.1
  1.6 0.9 copy-done.1
  2.5 0.0 copy-start.2
  2.5 0.9 copy-done.2
  3.5 0.0 copy-start.3
  3.5 0.9 copy-done.3
  4.4 0.0 copy-start.4
  4.4 0.9 copy-done.4
  5.4 0.0 copy-start.5
  5.4 0.9 copy-done.5
  6.3 0.0 copy-start.6
  6.3 0.9 copy-done.6
  7.2 0.0 copy-start.7
  7.2 0.9 copy-done.7
  8.1 0.0 copy-start.8
  8.1 0.9 copy-done.8
  9.1 0.0 copy-start.9
  9.1 0.9 copy-done.9
  10.0 0.0 copy-start.10
  10.0 0.9 copy-done.10
  10.9 0.0 copy-start.11
  10.9 0.8 copy-done.11
  11.7 0.7 copy-done.12
  12.4 0.7 copy-done.13
  13.1 0.7 copy-done.14
  13.8 0.7 copy-done.15
  14.5 102.5 %shard_map.175 = (f32[16,32,128]{2,1,0:T(8,128)S(1)}, f32[16,32,128]{2,1,0:T(8,128)S(1)}, f32[16,32,128]{2,1,0:T(8,128)S(1)}) custom-call(f32[16,32,128]{2,1,0:T(8,128)S(1)} %copy-done, f32[16,32,128]{2,1,0:T(8,128)S(1)} %copy-done.1, f32[16,32,128]{2,1,0:T(8,128)S(1)} %copy-done.2, s32[16,32,128]{2,1,0:T(8,128)S(1)} %copy-done.3, s32[32,128]{1,0:T(8,128)S(1)} %copy-done.12, ...), custom_call_target="tpu_custom_call" | custom-call | tf_op jit(solution)/shard_map/pallas_call | solution.py:433
  117.0 0.7 copy.22
  117.7 0.7 copy.23
  118.4 0.7 copy.24
  (4 shorter events, 0.0 us)
Async XLA Ops:
  0.6 1.0 copy-start
  1.6 0.9 copy-start.1
  2.5 0.9 copy-start.2
  3.5 0.9 copy-start.3
  4.4 0.9 copy-start.4
  5.4 0.9 copy-start.5
  6.3 0.9 copy-start.6
  7.2 0.9 copy-start.7
  8.1 0.9 copy-start.8
  9.1 0.9 copy-start.9
  10.0 0.9 copy-start.10
  10.9 0.8 copy-start.11
  11.7 0.7 copy-start.12
  12.4 0.7 copy-start.13
  13.1 0.7 copy-start.14
  13.8 0.7 copy-start.15

commit v2 on v1

--- a/solution.py
+++ b/solution.py
@@ -32,10 +32,13 @@
     safe = np.where(m == 0, 1.0, mu)
     gain = np.where(m == 0, 0.0, -1.0 / (2.0 * np.sinh(safe)))
     x = np.arange(LANES, dtype=np.float64)
-    rates = np.zeros((levels, LANES))
+    scan_e = np.zeros((7, levels, LANES))
+    scan_w = np.zeros((7, levels, LANES))
     for k in range(7):
-        rates[:, k] = np.exp(-mu * 2.0**k)
-    rates[:, 7] = gain
+        rate = np.exp(-mu * 2.0**k)[:, None]
+        scan_e[k] = np.where(x[None, :] >= 2**k, rate, 0.0)
+        scan_w[k] = np.where(x[None, :] < LANES - 2**k, rate, 0.0)
+    gain_full = np.broadcast_to(gain[:, None], (levels, LANES))
     phi_west = np.where(m[:, None] == 0, 1.0, gain[:, None] * np.exp(-mu[:, None] * (x + 1.0)))
     phi_east = np.where(m[:, None] == 0, x, gain[:, None] * np.exp(-mu[:, None] * (LANES - x)))
     near = 0.5 * np.abs(x[:, None] - x[None, :]) + x[:, None] * x[None, :] / columns
@@ -67,7 +70,7 @@
     haze_above = np.concatenate([np.cumsum(haze[::-1])[::-1], [0.0]])
     f32 = lambda a: np.ascontiguousarray(a, dtype=np.float32)
     return dict(
-        cosine=f32(cosine), cosine_t=f32(cosine.T), rates=f32(rates), phi_west=f32(phi_west),
+        cosine=f32(cosine), cosine_t=f32(cosine.T), scan_e=f32(scan_e), scan_w=f32(scan_w), gain=f32(gain_full), phi_west=f32(phi_west),
         phi_east=f32(phi_east), near=f32(near), direct=f32(direct), cross=f32(cross),
         haze=f32(haze_above),
     )
@@ -75,12 +78,18 @@
 
 def kernel(
     rows, heights,
-    u_hbm, w_hbm, t_hbm, class_ref, paved_ref, sun_ref, lookup_ref, haze_ref,
-    cosine_ref, cosine_t_ref, rates_ref, phi_w_ref, phi_e_ref, near_ref, direct_ref, cross_ref,
+    u_hbm, w_hbm, t_hbm, class_hbm, paved_hbm, sun_hbm, lookup_ref, haze_ref,
+    cosine_hbm, cosine_t_hbm, scan_e_hbm, scan_w_hbm, gain_hbm, phi_w_hbm, phi_e_hbm, near_hbm,
+    direct_hbm, cross_hbm,
+    un_hbm, wn_hbm, tn_hbm,
+    class_ref, paved_ref, sun_ref,
+    cosine_ref, cosine_t_ref, scan_e_ref, scan_w_ref, gain_ref, phi_w_ref, phi_e_ref, near_ref,
+    direct_ref, cross_ref,
     un_ref, wn_ref, tn_ref,
     ext, leaf, leaf_sum, leaf_in, side_out, side_in, side, us, ws, us_out, us_in,
     d_out, d_in, pm, mom, p_out, p_in, p_up, pc_out, pc_in,
-    in_sem, z_sem, side_sem, leaf_sem, star_sem, a2a_sem, mom_sem, back_sem, edge_sem,
+    in_sem, other_sem, out_sem,
+    z_sem, side_sem, leaf_sem, star_sem, a2a_sem, mom_sem, back_sem, edge_sem,
 ):
     r = lax.axis_index("row")
     h = lax.axis_index("height")
@@ -99,6 +108,16 @@
     ]
     for load in loads:
         load.start()
+    others = [
+        pltpu.make_async_copy(src, dst, other_sem.at[i])
+        for i, (src, dst) in enumerate((
+            (class_hbm, class_ref), (paved_hbm, paved_ref), (sun_hbm, sun_ref),
+            (cosine_hbm, cosine_ref), (scan_e_hbm, scan_e_ref), (scan_w_hbm, scan_w_ref),
+            (gain_hbm, gain_ref), (near_hbm, near_ref), (phi_w_hbm, phi_w_ref),
+            (phi_e_hbm, phi_e_ref), (direct_hbm, direct_ref), (cross_hbm, cross_ref),
+            (cosine_t_hbm, cosine_t_ref),
+        ))
+    ]
 
     barrier = pltpu.get_barrier_semaphore()
 
@@ -112,6 +131,8 @@
 
     lax.fori_loop(1, heights, greet_height, 0)
     lax.fori_loop(1, rows, greet_row, 0)
+    for copy in others:
+        copy.start()
     for load in loads:
         load.wait()
     lane = lax.broadcasted_iota(jnp.int32, (planes, LANES), 1)
@@ -124,7 +145,7 @@
             acc = jnp.where(mine, turned, acc)
         return acc
 
-    side_out[...] = lax.fori_loop(0, levels_here, pack_sides, jnp.zeros((planes, LANES), jnp.float32))
+    side_out[...] = lax.fori_loop(0, levels_here, pack_sides, jnp.zeros((planes, LANES), jnp.float32), unroll=True)
     pl.semaphore_wait(barrier, heights + rows - 2)
 
     def remote(src, dst, sems, slot, device):
@@ -141,6 +162,9 @@
     ]
     for copy in halo:
         copy.start()
+
+    for copy in others[:3]:
+        copy.wait()
 
     def leaf_level(z, total):
         classes = class_ref[z]
@@ -261,46 +285,54 @@
         return over, bottom
 
     lax.fori_loop(0, levels_here, heat, (over, first))
+    warm_out = pltpu.make_async_copy(tn_ref, tn_hbm, out_sem.at[2])
+    warm_out.start()
+    for copy in others[3:]:
+        copy.wait()
 
     finish(d_in, (heights - 1) * block, a2a_sem.at[1])
     grid = d_in[...].reshape(heights, 2, levels_here, LANES)
     both = jnp.concatenate([grid[:, 0].reshape(nz, LANES), grid[:, 1].reshape(nz, LANES)], axis=1)
     modes = jnp.dot(cosine_ref[...], both, precision=HIGHEST, preferred_element_type=jnp.float32)
-    pm[...] = modes
 
     lane8 = lax.broadcasted_iota(jnp.int32, (8, LANES), 1)
     sub8 = lax.broadcasted_iota(jnp.int32, (8, LANES), 0)
+    chunk = min(64, nz)
+    lane_c = lax.broadcasted_iota(jnp.int32, (chunk, LANES), 1)
 
     packed = jnp.zeros((8, LANES), jnp.float32)
     for y in range(2):
-        columns = pl.ds(y * LANES, LANES)
-
-        def scan_rows(g, acc, y=y, columns=columns):
-            at_rows = pl.ds(pl.multiple_of(g * 8, 8), 8)
-            d = pm[at_rows, columns]
-            rate = rates_ref[at_rows, :]
+        columns = slice(y * LANES, (y + 1) * LANES)
+        for start in range(0, nz, chunk):
+            part = slice(start, start + chunk)
+            d = modes[part, columns]
             fwd = d
             bwd = d
             for k in range(7):
                 s = 1 << k
-                rk = jnp.broadcast_to(rate[:, k : k + 1], (8, LANES))
-                fwd = fwd + rk * jnp.where(lane8 >= s, pltpu.roll(fwd, s, 1), 0.0)
-                bwd = bwd + rk * jnp.where(lane8 < LANES - s, pltpu.roll(bwd, LANES - s, 1), 0.0)
-            gain = jnp.broadcast_to(rate[:, 7:8], (8, LANES))
-            pm[at_rows, columns] = gain * (fwd + bwd - d)
-            j = 2 * (y * groups + g)
-            ends = jnp.where(lane8 == 0, bwd, fwd)
-            turned = pltpu.roll(ends, j, 1)
-            mine = (lane8 == j) | (lane8 == lax.rem(j + LANES - 1, LANES))
-            return jnp.where(mine, turned, acc)
-
-        zero = modes[0:8, y * LANES : (y + 1) * LANES]
-        packed = lax.fori_loop(0, groups, scan_rows, packed)
-        own = jnp.dot(zero, near_ref[...], precision=HIGHEST, preferred_element_type=jnp.float32)
-        pm[0:8, columns] = jnp.where(sub8 == 0, own, pm[0:8, columns])
-        first_moment = jnp.sum(zero * lane8.astype(jnp.float32), axis=1, keepdims=True)
-        slot = (sub8 == 0) & (lane8 == 2 * y * groups)
-        packed = jnp.where(slot, jnp.broadcast_to(first_moment, (8, LANES)), packed)
+                fwd = fwd + scan_e_ref[k, part, :] * pltpu.roll(fwd, s, 1)
+                bwd = bwd + scan_w_ref[k, part, :] * pltpu.roll(bwd, LANES - s, 1)
+            local = gain_ref[part, :] * (fwd + bwd - d)
+            ends = jnp.where(lane_c == 0, bwd, fwd)
+            if start == 0:
+                zero = d[0:8]
+                own = jnp.dot(
+                    zero, near_ref[...], precision=HIGHEST, preferred_element_type=jnp.float32
+                )
+                first_moment = jnp.sum(zero * lane8.astype(jnp.float32), axis=1, keepdims=True)
+                slot = (sub8 == 0) & (lane8 == 0)
+                pm[0:8, columns] = jnp.where(sub8 == 0, own, local[0:8])
+                pm[8:chunk, columns] = local[8:]
+            else:
+                pm[part, columns] = local
+            for i in range(chunk // 8):
+                value = ends[8 * i : 8 * i + 8]
+                if start == 0 and i == 0:
+                    value = jnp.where(slot, jnp.broadcast_to(first_moment, (8, LANES)), value)
+                j = 2 * (y * groups + start // 8 + i)
+                turned = pltpu.roll(value, j, 1) if j else value
+                mine = (lane8 == j) | (lane8 == (j + LANES - 1) % LANES)
+                packed = jnp.where(mine, turned, packed)
 
     mom[r] = packed
 
@@ -326,22 +358,16 @@
     )
 
     for y in range(2):
-        columns = pl.ds(y * LANES, LANES)
-
-        def add_inflow(g, c, y=y, columns=columns):
-            at_rows = pl.ds(pl.multiple_of(g * 8, 8), 8)
+        columns = slice(y * LANES, (y + 1) * LANES)
+        for g in range(groups):
+            part = slice(8 * g, 8 * g + 8)
             j = 2 * (y * groups + g)
-            turned = pltpu.roll(inflow, lax.rem(LANES - j, LANES), 1)
-            from_east = jnp.broadcast_to(turned[:, 0:1], (8, LANES))
-            from_west = jnp.broadcast_to(turned[:, LANES - 1 : LANES], (8, LANES))
-            pm[at_rows, columns] = (
-                pm[at_rows, columns]
-                + phi_w_ref[at_rows, :] * from_west
-                + phi_e_ref[at_rows, :] * from_east
+            west = (j + LANES - 1) % LANES
+            from_east = jnp.broadcast_to(inflow[:, j : j + 1], (8, LANES))
+            from_west = jnp.broadcast_to(inflow[:, west : west + 1], (8, LANES))
+            pm[part, columns] = (
+                pm[part, columns] + phi_w_ref[part, :] * from_west + phi_e_ref[part, :] * from_east
             )
-            return c
-
-        lax.fori_loop(0, groups, add_inflow, 0)
 
     solved = jnp.dot(cosine_t_ref[...], pm[...], precision=HIGHEST, preferred_element_type=jnp.float32)
     halves = [
@@ -377,6 +403,15 @@
         return above
 
     lax.fori_loop(0, levels_here, project, pc_out[1])
+    ends_out = [
+        pltpu.make_async_copy(un_ref, un_hbm, out_sem.at[0]),
+        pltpu.make_async_copy(wn_ref, wn_hbm, out_sem.at[1]),
+    ]
+    for copy in ends_out:
+        copy.start()
+    warm_out.wait()
+    for copy in ends_out:
+        copy.wait()
 
     finish(d_out, (heights - 1) * block, a2a_sem.at[0])
     finish(mom, rows - 1, mom_sem.at[0])
@@ -390,7 +425,6 @@
         levels_here, planes, width = u.shape
         nz = levels_here * heights
         table = tables(nz, width * rows, rows)
-        vmem = pl.BlockSpec(memory_space=pltpu.VMEM)
         smem = pl.BlockSpec(memory_space=pltpu.SMEM)
         hbm = pl.BlockSpec(memory_space=pl.ANY)
         field = jax.ShapeDtypeStruct(u.shape, jnp.float32)
@@ -400,9 +434,25 @@
         call = pl.pallas_call(
             functools.partial(kernel, rows, heights),
             out_shape=(field, field, field),
-            in_specs=[hbm] * 3 + [vmem] * 3 + [smem] * 2 + [vmem] * 8,
-            out_specs=(vmem, vmem, vmem),
+            in_specs=[hbm] * 6 + [smem] * 2 + [hbm] * 10,
+            out_specs=(hbm, hbm, hbm),
             scratch_shapes=[
+                pltpu.VMEM((levels_here,) + plane, jnp.int32),
+                pltpu.VMEM(plane, jnp.int32),
+                pltpu.VMEM(plane, f32),
+                pltpu.VMEM((nz, nz), f32),
+                pltpu.VMEM((nz, nz), f32),
+                pltpu.VMEM((7, nz, LANES), f32),
+                pltpu.VMEM((7, nz, LANES), f32),
+                pltpu.VMEM((nz, LANES), f32),
+                pltpu.VMEM((nz, LANES), f32),
+                pltpu.VMEM((nz, LANES), f32),
+                pltpu.VMEM((LANES, LANES), f32),
+                pltpu.VMEM((rows, 8, LANES), f32),
+                pltpu.VMEM((rows, 8, LANES), f32),
+                pltpu.VMEM(u.shape, f32),
+                pltpu.VMEM(u.shape, f32),
+                pltpu.VMEM(u.shape, f32),
                 pltpu.VMEM((3, levels_here + 2) + plane, f32),
                 pltpu.VMEM((levels_here,) + plane, f32),
                 pltpu.VMEM(plane, f32),
@@ -423,17 +473,17 @@
                 pltpu.VMEM(plane, f32),
                 pltpu.VMEM((2,) + plane, f32),
                 pltpu.VMEM(plane, f32),
-                dma((3,)), dma((2, 2)), dma((2, 2)), dma((2, 2)), dma((2, 2)),
+                dma((3,)), dma((13,)), dma((3,)), dma((2, 2)), dma((2, 2)), dma((2, 2)), dma((2, 2)),
                 dma((2,)), dma((2,)), dma((2,)), dma((2, 2)),
             ],
             compiler_params=pltpu.CompilerParams(
-                collective_id=0, has_side_effects=True, vmem_limit_bytes=32 * 1024 * 1024
+                collective_id=0, has_side_effects=True, vmem_limit_bytes=60 * 1024 * 1024
             ),
         )
         return call(
             u, w, t, classes, paved, sun, lookup, table["haze"], table["cosine"],
-            table["cosine_t"], table["rates"], table["phi_west"], table["phi_east"],
-            table["near"], table["direct"], table["cross"],
+            table["cosine_t"], table["scan_e"], table["scan_w"], table["gain"],
+            table["phi_west"], table["phi_east"], table["near"], table["direct"], table["cross"],
         )
 
     field = P("height", None, "row")

time: 120 us -> 63.4 us (0.53)
  Pallas kernels: 103 us -> 59.1 us
  local copies, waits for them, and re-layouts: 15.9 us -> 3.46 us
    pallas_call x1, Pallas kernels: 103 us -> 59.1 us  [per_device(): call(u, w, t, classes, paved, sun, lookup, table['haze'], table['cosine']...]
    unnamed x35 -> x7, local copies, waits for them, and re-layouts: 15.9 us -> 3.46 us
where the time goes in v2:
time: 63.4 us; the launch traced here: 63.2 us
  Pallas kernels  59.1 us (93%)
  local copies, waits for them, and re-layouts  3.46 us (5%)
  between operations  0.65 us (1%)
    pallas_call x1, Pallas kernels, per_device(): call(u, w, t, classes, paved, sun, lookup, table['haze'], table['cosine']...  59.1 us
    unnamed x7, local copies, waits for them, and re-layouts  3.46 us

profile of v2, /device:TPU:1, one launch (start us, length us, event | category | flops | bytes accessed | tf_op | source)
XLA Modules:
  0.0 63.2 jit_solution(13140362304874088717)
XLA Ops:
  0.6 59.1 %shard_map.193 = (f32[16,32,128]{2,1,0:T(8,128)}, f32[16,32,128]{2,1,0:T(8,128)}, f32[16,32,128]{2,1,0:T(8,128)}) custom-call(f32[16,32,128]{2,1,0:T(8,128)} %u_hbm.1, f32[16,32,128]{2,1,0:T(8,128)} %w_hbm.1, f32[16,32,128]{2,1,0:T(8,128)} %t_hbm.1, s32[16,32,128]{2,1,0:T(8,128)} %class_hbm.1, s32[32,128]{1,0:T(8,128)} %paved_hbm.1, f32[32,128]{1,0:T(8,128)} %sun_hbm.1, ...), custom_call_target="tpu_custom_call" | custom-call | tf_op jit(solution)/shard_map/pallas_call | solution.py:483
  59.8 0.0 copy-start.1
  59.8 1.7 %copy.24 = f32[16,32,128]{2,1,0:T(8,128)} copy(f32[16,32,128]{2,1,0:T(8,128)} %get-tuple-element.6) | data formatting | bytes 524288
  61.5 0.0 copy-done.1
  61.5 0.0 copy-start
  61.5 0.7 %copy.25 = f32[16,32,128]{2,1,0:T(8,128)} copy(f32[16,32,128]{2,1,0:T(8,128)S(1)} %copy-done.1) | data formatting | bytes 524288
  62.2 0.3 copy-done
  62.5 0.7 %copy.26 = f32[16,32,128]{2,1,0:T(8,128)} copy(f32[16,32,128]{2,1,0:T(8,128)S(1)} %copy-done) | data formatting | bytes 524288
Async XLA Ops:
  59.8 1.7 %copy-start.1 = (f32[16,32,128]{2,1,0:T(8,128)S(1)}, f32[16,32,128]{2,1,0:T(8,128)}, u32[]{:S(2)}) copy-start(f32[16,32,128]{2,1,0:T(8,128)} %get-tuple-element.7) | copy-start | bytes 786436
  61.5 1.0 %copy-start = (f32[16,32,128]{2,1,0:T(8,128)S(1)}, f32[16,32,128]{2,1,0:T(8,128)}, u32[]{:S(2)}) copy-start(f32[16,32,128]{2,1,0:T(8,128)} %get-tuple-element.8) | copy-start | bytes 786436

commit v3 on v2

--- a/solution.py
+++ b/solution.py
@@ -19,6 +19,7 @@
 PAVED_ABSORB = 0.9
 GRASS_ABSORB = 0.5
 MESH = pl.DeviceIdType.MESH
+UNROLL = True
 HIGHEST = lax.Precision.HIGHEST
 LANES = 128
 
@@ -42,6 +43,7 @@
     phi_west = np.where(m[:, None] == 0, 1.0, gain[:, None] * np.exp(-mu[:, None] * (x + 1.0)))
     phi_east = np.where(m[:, None] == 0, x, gain[:, None] * np.exp(-mu[:, None] * (LANES - x)))
     near = 0.5 * np.abs(x[:, None] - x[None, :]) + x[:, None] * x[None, :] / columns
+    near_next = np.broadcast_to((0.5 * (LANES - x) + LANES * x / columns)[:, None], (LANES, LANES))
     lane = np.arange(LANES)
     odd = lane % 2 == 1
     group = np.where(odd, (lane + 1) // 2, lane // 2) % 64
@@ -71,7 +73,7 @@
     f32 = lambda a: np.ascontiguousarray(a, dtype=np.float32)
     return dict(
         cosine=f32(cosine), cosine_t=f32(cosine.T), scan_e=f32(scan_e), scan_w=f32(scan_w), gain=f32(gain_full), phi_west=f32(phi_west),
-        phi_east=f32(phi_east), near=f32(near), direct=f32(direct), cross=f32(cross),
+        phi_east=f32(phi_east), near=f32(near), near_next=f32(near_next), direct=f32(direct), cross=f32(cross),
         haze=f32(haze_above),
     )
 
@@ -80,16 +82,16 @@
     rows, heights,
     u_hbm, w_hbm, t_hbm, class_hbm, paved_hbm, sun_hbm, lookup_ref, haze_ref,
     cosine_hbm, cosine_t_hbm, scan_e_hbm, scan_w_hbm, gain_hbm, phi_w_hbm, phi_e_hbm, near_hbm,
-    direct_hbm, cross_hbm,
-    un_hbm, wn_hbm, tn_hbm,
+    near_next_hbm, direct_hbm, cross_hbm,
+    us_hbm, ws_hbm, p_in, tn_hbm,
     class_ref, paved_ref, sun_ref,
     cosine_ref, cosine_t_ref, scan_e_ref, scan_w_ref, gain_ref, phi_w_ref, phi_e_ref, near_ref,
-    direct_ref, cross_ref,
-    un_ref, wn_ref, tn_ref,
-    ext, leaf, leaf_sum, leaf_in, side_out, side_in, side, us, ws, us_out, us_in,
-    d_out, d_in, pm, mom, p_out, p_in, p_up, pc_out, pc_in,
+    near_next_ref, direct_ref, cross_ref,
+    tn_ref,
+    ext, leaf, leaf_sum, leaf_in, low_out, low_in, side_out, side_in, side, u_side, us, ws,
+    d_out, d_in, pm, extra, mom, p_out,
     in_sem, other_sem, out_sem,
-    z_sem, side_sem, leaf_sem, star_sem, a2a_sem, mom_sem, back_sem, edge_sem,
+    z_sem, side_sem, leaf_sem, a2a_sem, mom_sem, back_sem,
 ):
     r = lax.axis_index("row")
     h = lax.axis_index("height")
@@ -102,19 +104,21 @@
     def at(dr, dh):
         return (lax.rem(r + dr + rows, rows), lax.rem(h + dh + heights, heights))
 
+    first_class = pltpu.make_async_copy(class_hbm, class_ref, other_sem.at[0])
     loads = [
         pltpu.make_async_copy(ref, ext.at[f, pl.ds(1, levels_here)], in_sem.at[f])
         for f, ref in enumerate((u_hbm, w_hbm, t_hbm))
     ]
     for load in loads:
         load.start()
+    first_class.start()
     others = [
-        pltpu.make_async_copy(src, dst, other_sem.at[i])
+        pltpu.make_async_copy(src, dst, other_sem.at[i + 1])
         for i, (src, dst) in enumerate((
-            (class_hbm, class_ref), (paved_hbm, paved_ref), (sun_hbm, sun_ref),
+            (paved_hbm, paved_ref), (sun_hbm, sun_ref),
             (cosine_hbm, cosine_ref), (scan_e_hbm, scan_e_ref), (scan_w_hbm, scan_w_ref),
             (gain_hbm, gain_ref), (near_hbm, near_ref), (phi_w_hbm, phi_w_ref),
-            (phi_e_hbm, phi_e_ref), (direct_hbm, direct_ref), (cross_hbm, cross_ref),
+            (phi_e_hbm, phi_e_ref), (near_next_hbm, near_next_ref), (direct_hbm, direct_ref), (cross_hbm, cross_ref),
             (cosine_t_hbm, cosine_t_ref),
         ))
     ]
@@ -131,22 +135,37 @@
 
     lax.fori_loop(1, heights, greet_height, 0)
     lax.fori_loop(1, rows, greet_row, 0)
+    corners = (at(1, 1), at(1, -1), at(-1, 1))
+    for corner in (*corners, at(-1, -1)):
+        pl.semaphore_signal(barrier, inc=1, device_id=corner, device_id_type=MESH)
     for copy in others:
         copy.start()
     for load in loads:
         load.wait()
     lane = lax.broadcasted_iota(jnp.int32, (planes, LANES), 1)
 
+    def leaf_of(classes):
+        area = jnp.zeros((planes, LANES), jnp.float32)
+        for c in range(lookup_ref.shape[0]):
+            area = jnp.where(classes == c, lookup_ref[c], area)
+        return area
+
     def pack_sides(z, acc):
         for f in range(3):
             j = 2 * (f * levels_here + z)
-            turned = pltpu.roll(ext[f, z + 1], j, 1)
-            mine = (lane == j) | (lane == lax.rem(j + LANES - 1, LANES))
-            acc = jnp.where(mine, turned, acc)
-        return acc
-
+            turned = pltpu.roll(ext[f, z + 1], j + 1, 1)
+            acc = jnp.where((lane == j) | (lane == j + 1), turned, acc)
+        j = 6 * levels_here + 2 * z
+        turned = pltpu.roll(ext[0, z + 1], lax.rem(j + 2, LANES), 1)
+        acc = jnp.where(lane == j, turned, acc)
+        turned = pltpu.roll(class_ref[z].astype(jnp.float32), lax.rem(j + 2, LANES), 1)
+        return jnp.where(lane == j + 1, turned, acc)
+
+    first_class.wait()
     side_out[...] = lax.fori_loop(0, levels_here, pack_sides, jnp.zeros((planes, LANES), jnp.float32), unroll=True)
-    pl.semaphore_wait(barrier, heights + rows - 2)
+    low_out[0] = ext[1, levels_here - 1]
+    low_out[1] = leaf_of(class_ref[levels_here - 1])
+    pl.semaphore_wait(barrier, heights + rows + 2)
 
     def remote(src, dst, sems, slot, device):
         return pltpu.make_async_remote_copy(
@@ -159,23 +178,20 @@
         remote(side_out, side_in.at[1], side_sem, 1, at(-1, 0)),
         remote(ext.at[:, levels_here], ext.at[:, 0], z_sem, 0, at(0, 1)),
         remote(ext.at[:, 1], ext.at[:, levels_here + 1], z_sem, 1, at(0, -1)),
+        remote(low_out, low_in, z_sem, 2, at(0, 1)),
+    ] + [
+        remote(side_out, side_in.at[2 + i], side_sem, 2 + i, corner) for i, corner in enumerate(corners)
     ]
     for copy in halo:
         copy.start()
 
-    for copy in others[:3]:
-        copy.wait()
-
     def leaf_level(z, total):
-        classes = class_ref[z]
-        area = jnp.zeros((planes, LANES), jnp.float32)
-        for c in range(lookup_ref.shape[0]):
-            area = jnp.where(classes == c, lookup_ref[c], area)
+        area = leaf_of(class_ref[z])
         area = jnp.where(h * levels_here + z < CANOPY, area, 0.0)
         leaf[z] = area
         return total + area
 
-    leaf_sum[...] = lax.fori_loop(0, levels_here, leaf_level, jnp.zeros((planes, LANES), jnp.float32))
+    leaf_sum[...] = lax.fori_loop(0, levels_here, leaf_level, jnp.zeros((planes, LANES), jnp.float32), unroll=UNROLL)
     leaf_copies = [
         remote(leaf_sum, leaf_in.at[0], leaf_sem, 0, at(0, -1)),
         remote(leaf_sum, leaf_in.at[1], leaf_sem, 1, at(0, -2)),
@@ -195,54 +211,71 @@
         ext[:, levels_here + 1] = jnp.zeros((3, planes, LANES), jnp.float32)
 
     even = lax.rem(lane, 2) == 0
-    side[...] = jnp.where(even, pltpu.roll(side_in[0], 1, 1), pltpu.roll(side_in[1], LANES - 1, 1))
+    from_left = side_in[0]
+    side[...] = jnp.where(even, pltpu.roll(side_in[1], LANES - 1, 1), pltpu.roll(from_left, 1, 1))
+
+    def stretch(q, u, w, east, west, above, below):
+        advect = u * (east - west) * 0.5 + w * (above - below) * 0.5
+        diffuse = VISCOSITY * (east + west + above + below - 4.0 * q)
+        return diffuse - advect
+
+    def drag(area, u, w):
+        return DRAG_COEF * area * jnp.sqrt(u * u + w * w + SPAN_VAR)
+
+    last = 2 * (levels_here - 1)
+    w_left = pltpu.roll(from_left, LANES - 2 * levels_here, 1)
+    u_far = pltpu.roll(from_left, LANES - 6 * levels_here, 1)
+    class_left = pltpu.roll(from_left, LANES - 6 * levels_here - 1, 1)
+    z_of_lane = h * levels_here + lane // 2
+    area_left = jnp.where(z_of_lane < CANOPY, leaf_of(class_left), 0.0)
+    u_east = pltpu.roll(side_out[...], LANES - 1, 1)
+    corner_above = jnp.where(h < heights - 1, pltpu.roll(side_in[3], last, 1), 0.0)
+    corner_below = jnp.where(h > 0, pltpu.roll(side_in[2], LANES - last, 1), 0.0)
+    u_above = jnp.where(lane == last, corner_above, pltpu.roll(from_left, LANES - 2, 1))
+    u_below = jnp.where(lane == 0, corner_below, pltpu.roll(from_left, 2, 1))
+    u_side[...] = from_left + DT * (
+        stretch(from_left, from_left, w_left, u_east, u_far, u_above, u_below)
+        - drag(area_left, from_left, w_left) * from_left
+    )
+
+    u_low, w_low, t_low = ext[0, 0], ext[1, 0], ext[2, 0]
+    j = 2 * (2 * levels_here - 1)
+    w_east = jnp.where(
+        lane == LANES - 1, pltpu.roll(side_in[4], LANES - 2 - j, 1), pltpu.roll(w_low, LANES - 1, 1)
+    )
+    w_west = jnp.where(lane == 0, pltpu.roll(side_in[2], LANES - j, 1), pltpu.roll(w_low, 1, 1))
+    area_low = jnp.where(h * levels_here - 1 < CANOPY, low_in[1], 0.0)
+    w_star_low = w_low + DT * (
+        stretch(w_low, u_low, w_low, w_east, w_west, ext[1, 1], low_in[0])
+        - drag(area_low, u_low, w_low) * w_low
+        + THERMAL_LIFT * t_low
+    )
+    w_star_low = jnp.where(h > 0, w_star_low, 0.0)
 
     def growth(f, z, u, w):
         q = ext[f, z + 1]
         j = 2 * (f * levels_here + z)
-        edge = pltpu.roll(side[...], lax.rem(LANES - j, LANES), 1)
+        edge = pltpu.roll(side[...], LANES - 1 - j, 1)
         east = jnp.where(lane == LANES - 1, edge, pltpu.roll(q, LANES - 1, 1))
         west = jnp.where(lane == 0, edge, pltpu.roll(q, 1, 1))
-        above = ext[f, z + 2]
-        below = ext[f, z]
-        advect = u * (east - west) * 0.5 + w * (above - below) * 0.5
-        diffuse = VISCOSITY * (east + west + above + below - 4.0 * q)
-        return diffuse - advect
-
-    def winds(z, acc):
+        return stretch(q, u, w, east, west, ext[f, z + 2], ext[f, z])
+
+    def winds(z, w_below):
         u = ext[0, z + 1]
         w = ext[1, z + 1]
         t = ext[2, z + 1]
-        friction = DRAG_COEF * leaf[z] * jnp.sqrt(u * u + w * w + SPAN_VAR)
+        friction = drag(leaf[z], u, w)
         u_star = u + DT * (growth(0, z, u, w) - friction * u)
         w_star = w + DT * (growth(1, z, u, w) - friction * w + THERMAL_LIFT * t)
         w_star = jnp.where(h * levels_here + z == nz - 1, 0.0, w_star)
         us[z] = u_star
-        ws[z + 1] = w_star
-        return jnp.where(lane == z, pltpu.roll(u_star, z + 1, 1), acc)
-
-    us_out[...] = lax.fori_loop(0, levels_here, winds, jnp.zeros((planes, LANES), jnp.float32))
-    star = [
-        remote(us_out, us_in, star_sem, 0, at(1, 0)),
-        remote(ws.at[levels_here], ws.at[0], star_sem, 1, at(0, 1)),
-    ]
-    for copy in star:
-        copy.start()
-    for copy in star:
-        copy.wait()
-
-    @pl.when(h == 0)
-    def _():
-        ws[0] = jnp.zeros((planes, LANES), jnp.float32)
-
-    def divergence(z, c):
-        u_star = us[z]
-        edge = pltpu.roll(us_in[...], lax.rem(LANES - z, LANES), 1)
+        ws[z] = w_star
+        edge = pltpu.roll(u_side[...], lax.rem(LANES - 2 * z, LANES), 1)
         west = jnp.where(lane == 0, edge, pltpu.roll(u_star, 1, 1))
-        d_out[pl.ds(z, planes, stride=levels_here), :] = u_star - west + (ws[z + 1] - ws[z])
-        return c
-
-    lax.fori_loop(0, levels_here, divergence, 0)
+        d_out[pl.ds(z, planes, stride=levels_here), :] = u_star - west + (w_star - w_below)
+        return w_star
+
+    lax.fori_loop(0, levels_here, winds, w_star_low, unroll=UNROLL)
 
     def exchange(out, into, sems):
         def send(i, c):
@@ -263,6 +296,14 @@
         pltpu.make_async_copy(part, part, sem).wait()
 
     exchange(d_out, d_in, a2a_sem)
+    star_out = [
+        pltpu.make_async_copy(us, us_hbm, out_sem.at[0]),
+        pltpu.make_async_copy(ws, ws_hbm, out_sem.at[1]),
+    ]
+    for copy in star_out:
+        copy.start()
+    for copy in others[:2]:
+        copy.wait()
 
     for copy in leaf_copies:
         copy.wait()
@@ -284,10 +325,10 @@
         tn_ref[z] = t + DT * (growth(2, z, ext[0, z + 1], ext[1, z + 1]) + warming)
         return over, bottom
 
-    lax.fori_loop(0, levels_here, heat, (over, first))
+    lax.fori_loop(0, levels_here, heat, (over, first), unroll=UNROLL)
     warm_out = pltpu.make_async_copy(tn_ref, tn_hbm, out_sem.at[2])
     warm_out.start()
-    for copy in others[3:]:
+    for copy in others[2:]:
         copy.wait()
 
     finish(d_in, (heights - 1) * block, a2a_sem.at[1])
@@ -301,6 +342,7 @@
     lane_c = lax.broadcasted_iota(jnp.int32, (chunk, LANES), 1)
 
     packed = jnp.zeros((8, LANES), jnp.float32)
+    own_next = []
     for y in range(2):
         columns = slice(y * LANES, (y + 1) * LANES)
         for start in range(0, nz, chunk):
@@ -319,6 +361,9 @@
                 own = jnp.dot(
                     zero, near_ref[...], precision=HIGHEST, preferred_element_type=jnp.float32
                 )
+                own_next.append(jnp.dot(
+                    zero, near_next_ref[...], precision=HIGHEST, preferred_element_type=jnp.float32
+                ))
                 first_moment = jnp.sum(zero * lane8.astype(jnp.float32), axis=1, keepdims=True)
                 slot = (sub8 == 0) & (lane8 == 0)
                 pm[0:8, columns] = jnp.where(sub8 == 0, own, local[0:8])
@@ -357,65 +402,109 @@
         lax.rem(lane8, 2) == 0, pltpu.roll(cross, 1, 1), pltpu.roll(cross, LANES - 1, 1)
     )
 
-    for y in range(2):
-        columns = slice(y * LANES, (y + 1) * LANES)
-        for g in range(groups):
-            part = slice(8 * g, 8 * g + 8)
+    for g in range(groups):
+        part = slice(8 * g, 8 * g + 8)
+        rate, gain = scan_w_ref[0, part, :], gain_ref[part, :]
+        next_columns = []
+        for y in range(2):
+            columns = slice(y * LANES, (y + 1) * LANES)
             j = 2 * (y * groups + g)
             west = (j + LANES - 1) % LANES
             from_east = jnp.broadcast_to(inflow[:, j : j + 1], (8, LANES))
             from_west = jnp.broadcast_to(inflow[:, west : west + 1], (8, LANES))
-            pm[part, columns] = (
-                pm[part, columns] + phi_w_ref[part, :] * from_west + phi_e_ref[part, :] * from_east
-            )
-
+            onward = pm[part, columns] + phi_w_ref[part, :] * from_west
+            pm[part, columns] = onward + phi_e_ref[part, :] * from_east
+            beyond = rate * jnp.broadcast_to(onward[:, LANES - 1 :], (8, LANES)) + gain * from_east
+            if g == 0:
+                beyond = jnp.where(
+                    sub8 == 0, own_next[y] + from_west + float(LANES) * from_east, beyond
+                )
+            next_columns.append(beyond)
+        extra[part, :] = jnp.where(lane8 == 0, next_columns[0], next_columns[1])
+
+    beyond = jnp.dot(
+        jnp.transpose(extra[...])[0:8], cosine_ref[...],
+        precision=HIGHEST, preferred_element_type=jnp.float32,
+    )
     solved = jnp.dot(cosine_t_ref[...], pm[...], precision=HIGHEST, preferred_element_type=jnp.float32)
-    halves = [
-        solved[:, y * LANES : (y + 1) * LANES].reshape(heights, 1, levels_here, LANES) for y in range(2)
-    ]
-    p_out[...] = jnp.concatenate(halves, axis=1).reshape(nz * 2, LANES)
-    exchange(p_out, p_in, back_sem)
-    finish(p_in, (heights - 1) * block, back_sem.at[1])
-
-    def first_columns(z, acc):
-        p = p_in[pl.ds(z, planes, stride=levels_here), :]
-        return jnp.where(lane == z, pltpu.roll(p, z, 1), acc)
-
-    pc_out[0] = lax.fori_loop(0, levels_here, first_columns, jnp.zeros((planes, LANES), jnp.float32))
-    pc_out[1] = p_in[pl.ds(0, planes, stride=levels_here), :]
-    edges = [
-        remote(pc_out.at[0], pc_in, edge_sem, 0, at(-1, 0)),
-        remote(pc_out.at[1], p_up, edge_sem, 1, at(0, -1)),
-    ]
-    for copy in edges:
-        copy.start()
-    for copy in edges:
-        copy.wait()
-
-    def project(z, p):
-        edge = pltpu.roll(pc_in[...], LANES - 1 - z, 1)
-        east = jnp.where(lane == LANES - 1, edge, pltpu.roll(p, LANES - 1, 1))
-        un_ref[z] = us[z] - (east - p)
-        inside = p_in[pl.ds(jnp.minimum(z + 1, levels_here - 1), planes, stride=levels_here), :]
-        above = jnp.where(z == levels_here - 1, p_up[...], inside)
-        rise = jnp.where(h * levels_here + z == nz - 1, 0.0, above - p)
-        wn_ref[z] = ws[z + 1] - rise
-        return above
-
-    lax.fori_loop(0, levels_here, project, pc_out[1])
-    ends_out = [
-        pltpu.make_async_copy(un_ref, un_hbm, out_sem.at[0]),
-        pltpu.make_async_copy(wn_ref, wn_hbm, out_sem.at[1]),
-    ]
-    for copy in ends_out:
-        copy.start()
-    warm_out.wait()
-    for copy in ends_out:
-        copy.wait()
-
+    tall = levels_here + 4
+    for to in range(heights):
+        z0 = to * levels_here
+        half = z0 // LANES
+        for y in range(2):
+            base = (2 * to + y) * tall
+            columns = slice(y * LANES, (y + 1) * LANES)
+            top = min(z0 + levels_here, nz - 1)
+            p_out[base : base + levels_here] = solved[z0 : z0 + levels_here, columns]
+            p_out[base + levels_here : base + levels_here + 1] = solved[top : top + 1, columns]
+            p_out[base + levels_here + 1 : base + levels_here + 2] = beyond[
+                y : y + 1, half * LANES : (half + 1) * LANES
+            ]
+
+    def send_back(i, c):
+        to = lax.rem(h + i, heights)
+        pltpu.make_async_remote_copy(
+            src_ref=p_out.at[pl.ds(to * 2 * tall, 2 * tall)],
+            dst_ref=p_in.at[pl.ds(h * 2 * tall, 2 * tall)],
+            send_sem=back_sem.at[0], recv_sem=back_sem.at[1],
+            device_id=(r, to), device_id_type=MESH,
+        ).start()
+        return c
+
+    lax.fori_loop(1, heights, send_back, 0)
+    mine = pl.ds(h * 2 * tall, 2 * tall)
+    own_block = pltpu.make_async_copy(p_out.at[mine], p_in.at[mine], out_sem.at[3])
+    own_block.start()
     finish(d_out, (heights - 1) * block, a2a_sem.at[0])
     finish(mom, rows - 1, mom_sem.at[0])
-    finish(p_out, (heights - 1) * block, back_sem.at[0])
+    warm_out.wait()
+    for copy in star_out:
+        copy.wait()
+    own_block.wait()
+    finish(p_in, (heights - 1) * 2 * tall, back_sem.at[1])
+    finish(p_out, (heights - 1) * 2 * tall, back_sem.at[0])
+
+
+def project_kernel(
+    heights, us_hbm, ws_hbm, p_hbm, warm_hbm, un_hbm, wn_hbm, tn_hbm,
+    us, ws, p_in, warm, un, wn, in_sem, out_sem,
+):
+    loads = [
+        pltpu.make_async_copy(src, dst, in_sem.at[i])
+        for i, (src, dst) in enumerate(((warm_hbm, warm), (p_hbm, p_in), (us_hbm, us), (ws_hbm, ws)))
+    ]
+    for load in loads:
+        load.start()
+    h = lax.axis_index("height")
+    levels_here, planes = us.shape[0], us.shape[1]
+    tall = levels_here + 4
+    lane = lax.broadcasted_iota(jnp.int32, (planes, LANES), 1)
+    loads[0].wait()
+    warm_out = pltpu.make_async_copy(warm, tn_hbm, out_sem.at[2])
+    warm_out.start()
+    for load in loads[1:]:
+        load.wait()
+    beyond = p_in[pl.ds(levels_here + 1, planes, stride=tall), :]
+    first = lax.rem(h * levels_here, LANES)
+
+    def project(z, p):
+        edge = pltpu.roll(beyond, LANES - 1 - first - z, 1)
+        east = jnp.where(lane == LANES - 1, edge, pltpu.roll(p, LANES - 1, 1))
+        un[z] = us[z] - (east - p)
+        above = p_in[pl.ds(z + 1, planes, stride=tall), :]
+        wn[z] = ws[z] - (above - p)
+        return above
+
+    lax.fori_loop(0, levels_here, project, p_in[pl.ds(0, planes, stride=tall), :], unroll=UNROLL)
+    stores = [
+        pltpu.make_async_copy(un, un_hbm, out_sem.at[0]),
+        pltpu.make_async_copy(wn, wn_hbm, out_sem.at[1]),
+    ]
+    for store in stores:
+        store.start()
+    warm_out.wait()
+    for store in stores:
+        store.wait()
 
 
 def solution(mesh):
@@ -433,9 +522,9 @@
         dma = pltpu.SemaphoreType.DMA
         call = pl.pallas_call(
             functools.partial(kernel, rows, heights),
-            out_shape=(field, field, field),
-            in_specs=[hbm] * 6 + [smem] * 2 + [hbm] * 10,
-            out_specs=(hbm, hbm, hbm),
+            out_shape=(field, field, jax.ShapeDtypeStruct((2 * heights * (levels_here + 4), LANES), f32), field),
+            in_specs=[hbm] * 6 + [smem] * 2 + [hbm] * 11,
+            out_specs=(hbm,) * 4,
             scratch_shapes=[
                 pltpu.VMEM((levels_here,) + plane, jnp.int32),
                 pltpu.VMEM(plane, jnp.int32),
@@ -448,43 +537,54 @@
                 pltpu.VMEM((nz, LANES), f32),
                 pltpu.VMEM((nz, LANES), f32),
                 pltpu.VMEM((LANES, LANES), f32),
+                pltpu.VMEM((LANES, LANES), f32),
                 pltpu.VMEM((rows, 8, LANES), f32),
                 pltpu.VMEM((rows, 8, LANES), f32),
-                pltpu.VMEM(u.shape, f32),
-                pltpu.VMEM(u.shape, f32),
                 pltpu.VMEM(u.shape, f32),
                 pltpu.VMEM((3, levels_here + 2) + plane, f32),
                 pltpu.VMEM((levels_here,) + plane, f32),
                 pltpu.VMEM(plane, f32),
                 pltpu.VMEM((2,) + plane, f32),
-                pltpu.VMEM(plane, f32),
+                pltpu.VMEM((2,) + plane, f32),
                 pltpu.VMEM((2,) + plane, f32),
                 pltpu.VMEM(plane, f32),
-                pltpu.VMEM((levels_here,) + plane, f32),
-                pltpu.VMEM((levels_here + 1,) + plane, f32),
+                pltpu.VMEM((5,) + plane, f32),
                 pltpu.VMEM(plane, f32),
                 pltpu.VMEM(plane, f32),
+                pltpu.VMEM(u.shape, f32),
+                pltpu.VMEM(u.shape, f32),
                 pltpu.VMEM((2 * nz, LANES), f32),
                 pltpu.VMEM((2 * nz, LANES), f32),
                 pltpu.VMEM((nz, 2 * LANES), f32),
+                pltpu.VMEM((nz, LANES), f32),
                 pltpu.VMEM((rows, 8, LANES), f32),
-                pltpu.VMEM((2 * nz, LANES), f32),
-                pltpu.VMEM((2 * nz, LANES), f32),
-                pltpu.VMEM(plane, f32),
-                pltpu.VMEM((2,) + plane, f32),
-                pltpu.VMEM(plane, f32),
-                dma((3,)), dma((13,)), dma((3,)), dma((2, 2)), dma((2, 2)), dma((2, 2)), dma((2, 2)),
-                dma((2,)), dma((2,)), dma((2,)), dma((2, 2)),
+                pltpu.VMEM((2 * heights * (levels_here + 4), LANES), f32),
+                dma((3,)), dma((14,)), dma((4,)), dma((2, 3)), dma((2, 5)), dma((2, 2)),
+                dma((2,)), dma((2,)), dma((2,)),
             ],
             compiler_params=pltpu.CompilerParams(
                 collective_id=0, has_side_effects=True, vmem_limit_bytes=60 * 1024 * 1024
             ),
         )
-        return call(
+        us, ws, p, warm = call(
             u, w, t, classes, paved, sun, lookup, table["haze"], table["cosine"],
             table["cosine_t"], table["scan_e"], table["scan_w"], table["gain"],
-            table["phi_west"], table["phi_east"], table["near"], table["direct"], table["cross"],
+            table["phi_west"], table["phi_east"], table["near"], table["near_next"],
+            table["direct"], table["cross"],
         )
+        project = pl.pallas_call(
+            functools.partial(project_kernel, heights),
+            out_shape=(field, field, field),
+            in_specs=[hbm] * 4,
+            out_specs=(hbm,) * 3,
+            scratch_shapes=[
+                pltpu.VMEM(u.shape, f32), pltpu.VMEM(u.shape, f32), pltpu.VMEM(p.shape, f32),
+                pltpu.VMEM(u.shape, f32), pltpu.VMEM(u.shape, f32), pltpu.VMEM(u.shape, f32),
+                dma((4,)), dma((3,)),
+            ],
+            compiler_params=pltpu.CompilerParams(vmem_limit_bytes=60 * 1024 * 1024),
+        )
+        return project(us, ws, p, warm)
 
     field = P("height", None, "row")
     line = P(None, "row")

time: 63.4 us -> 53.7 us (0.85)
  Pallas kernels: 59.1 us -> 52.9 us
  local copies, waits for them, and re-layouts: 3.46 us -> 0 us
    pallas_call x1, Pallas kernels: 59.1 us -> 50.6 us  [per_device(): call(u, w, t, classes, paved, sun, lookup, table['haze'], table['cosine']...]
    unnamed x7 -> x0, local copies, waits for them, and re-layouts: 3.46 us -> none
    pallas_call x0 -> x1, Pallas kernels: none -> 2.26 us  [per_device(): return project(us, ws, p, warm)]
where the time goes in v3:
time: 53.7 us; the launch traced here: 53.5 us
  Pallas kernels  52.9 us (99%)
  between operations  0.64 us (1%)
    pallas_call x1, Pallas kernels, per_device(): call(u, w, t, classes, paved, sun, lookup, table['haze'], table['cosine']...  50.6 us
    pallas_call x1, Pallas kernels, per_device(): return project(us, ws, p, warm)  2.26 us

profile of v3, /device:TPU:1, one launch (start us, length us, event | category | flops | bytes accessed | tf_op | source)
XLA Modules:
  0.0 53.5 jit_solution(2255599225655028000)
XLA Ops:
  0.6 50.6 %shard_map.202 = (f32[16,32,128]{2,1,0:T(8,128)}, f32[16,32,128]{2,1,0:T(8,128)}, f32[640,128]{1,0:T(8,128)}, f32[16,32,128]{2,1,0:T(8,128)}) custom-call(f32[16,32,128]{2,1,0:T(8,128)} %u_hbm.1, f32[16,32,128]{2,1,0:T(8,128)} %w_hbm.1, f32[16,32,128]{2,1,0:T(8,128)} %t_hbm.1, s32[16,32,128]{2,1,0:T(8,128)} %class_hbm.1, s32[32,128]{1,0:T(8,128)} %paved_hbm.1, ...), custom_call_target="tpu_custom_call" | custom-call | tf_op jit(solution)/shard_map/pallas_call | solution.py:569
  51.3 2.3 %shard_map.203 = (f32[16,32,128]{2,1,0:T(8,128)}, f32[16,32,128]{2,1,0:T(8,128)}, f32[16,32,128]{2,1,0:T(8,128)}) custom-call(f32[16,32,128]{2,1,0:T(8,128)} %get-tuple-element.7.us_hbm, f32[16,32,128]{2,1,0:T(8,128)} %get-tuple-element.8.ws_hbm, f32[640,128]{1,0:T(8,128)} %get-tuple-element.9.p_hbm, f32[16,32,128]{2,1,0:T(8,128)} %get-tuple-element.10.warm_hbm), custom_call_target="tpu_custom_call" | custom-call | tf_op jit(solution)/shard_map/pallas_call | solution.py:587

commit v4 on v3

--- a/solution.py
+++ b/solution.py
@@ -20,6 +20,8 @@
 GRASS_ABSORB = 0.5
 MESH = pl.DeviceIdType.MESH
 UNROLL = True
+TALL = 18
+SLOT = 24
 HIGHEST = lax.Precision.HIGHEST
 LANES = 128
 
@@ -277,25 +279,27 @@
 
     lax.fori_loop(0, levels_here, winds, w_star_low, unroll=UNROLL)
 
-    def exchange(out, into, sems):
-        def send(i, c):
+    def finish(buffer, count, sem):
+        part = buffer.at[pl.ds(0, count)]
+        pltpu.make_async_copy(part, part, sem).wait()
+
+    for y in range(2):
+
+        def send_plane(i, c, y=y):
             to = lax.rem(h + i, heights)
             pltpu.make_async_remote_copy(
-                src_ref=out.at[pl.ds(to * block, block)], dst_ref=into.at[pl.ds(h * block, block)],
-                send_sem=sems.at[0], recv_sem=sems.at[1],
+                src_ref=d_out.at[pl.ds((2 * to + y) * levels_here, levels_here)],
+                dst_ref=d_in.at[y, pl.ds(h * levels_here, levels_here)],
+                send_sem=a2a_sem.at[0], recv_sem=a2a_sem.at[1 + y],
                 device_id=(r, to), device_id_type=MESH,
             ).start()
             return c
 
-        lax.fori_loop(1, heights, send, 0)
-        mine = pl.ds(h * block, block)
-        into[mine] = out[mine]
-
-    def finish(buffer, count, sem):
-        part = buffer.at[pl.ds(0, count)]
-        pltpu.make_async_copy(part, part, sem).wait()
-
-    exchange(d_out, d_in, a2a_sem)
+        lax.fori_loop(1, heights, send_plane, 0)
+    for y in range(2):
+        d_in[y, pl.ds(h * levels_here, levels_here)] = d_out[
+            pl.ds((2 * h + y) * levels_here, levels_here)
+        ]
     star_out = [
         pltpu.make_async_copy(us, us_hbm, out_sem.at[0]),
         pltpu.make_async_copy(ws, ws_hbm, out_sem.at[1]),
@@ -331,23 +335,21 @@
     for copy in others[2:]:
         copy.wait()
 
-    finish(d_in, (heights - 1) * block, a2a_sem.at[1])
-    grid = d_in[...].reshape(heights, 2, levels_here, LANES)
-    both = jnp.concatenate([grid[:, 0].reshape(nz, LANES), grid[:, 1].reshape(nz, LANES)], axis=1)
-    modes = jnp.dot(cosine_ref[...], both, precision=HIGHEST, preferred_element_type=jnp.float32)
-
     lane8 = lax.broadcasted_iota(jnp.int32, (8, LANES), 1)
     sub8 = lax.broadcasted_iota(jnp.int32, (8, LANES), 0)
     chunk = min(64, nz)
     lane_c = lax.broadcasted_iota(jnp.int32, (chunk, LANES), 1)
-
-    packed = jnp.zeros((8, LANES), jnp.float32)
-    own_next = []
-    for y in range(2):
-        columns = slice(y * LANES, (y + 1) * LANES)
+    slot = (sub8 == 0) & (lane8 == 0)
+
+    def row_scans(y):
+        finish(d_in.at[y], (heights - 1) * levels_here, a2a_sem.at[1 + y])
+        modes = jnp.dot(
+            cosine_ref[...], d_in[y], precision=HIGHEST, preferred_element_type=jnp.float32
+        )
+        packed = jnp.zeros((8, LANES), jnp.float32)
         for start in range(0, nz, chunk):
             part = slice(start, start + chunk)
-            d = modes[part, columns]
+            d = modes[part]
             fwd = d
             bwd = d
             for k in range(7):
@@ -361,108 +363,110 @@
                 own = jnp.dot(
                     zero, near_ref[...], precision=HIGHEST, preferred_element_type=jnp.float32
                 )
-                own_next.append(jnp.dot(
+                own_next = jnp.dot(
                     zero, near_next_ref[...], precision=HIGHEST, preferred_element_type=jnp.float32
-                ))
+                )
                 first_moment = jnp.sum(zero * lane8.astype(jnp.float32), axis=1, keepdims=True)
-                slot = (sub8 == 0) & (lane8 == 0)
-                pm[0:8, columns] = jnp.where(sub8 == 0, own, local[0:8])
-                pm[8:chunk, columns] = local[8:]
+                pm[y, 0:8] = jnp.where(sub8 == 0, own, local[0:8])
+                pm[y, 8:chunk] = local[8:]
             else:
-                pm[part, columns] = local
+                pm[y, part] = local
             for i in range(chunk // 8):
                 value = ends[8 * i : 8 * i + 8]
                 if start == 0 and i == 0:
                     value = jnp.where(slot, jnp.broadcast_to(first_moment, (8, LANES)), value)
-                j = 2 * (y * groups + start // 8 + i)
+                j = 2 * (start // 8 + i)
                 turned = pltpu.roll(value, j, 1) if j else value
                 mine = (lane8 == j) | (lane8 == (j + LANES - 1) % LANES)
                 packed = jnp.where(mine, turned, packed)
-
-    mom[r] = packed
-
-    def send_moments(i, c):
-        pltpu.make_async_remote_copy(
-            src_ref=mom.at[r], dst_ref=mom.at[r], send_sem=mom_sem.at[0], recv_sem=mom_sem.at[1],
-            device_id=at(i, 0), device_id_type=MESH,
-        ).start()
-        return c
-
-    lax.fori_loop(1, rows, send_moments, 0)
-    finish(mom, rows - 1, mom_sem.at[1])
-
-    def gather_moments(i, state):
-        direct, cross = state
-        values = mom[lax.rem(r + i, rows)]
-        return direct + direct_ref[i] * values, cross + cross_ref[i] * values
-
-    nothing = jnp.zeros((8, LANES), jnp.float32)
-    direct, cross = lax.fori_loop(0, rows, gather_moments, (nothing, nothing))
-    inflow = direct + jnp.where(
-        lax.rem(lane8, 2) == 0, pltpu.roll(cross, 1, 1), pltpu.roll(cross, LANES - 1, 1)
-    )
-
-    for g in range(groups):
-        part = slice(8 * g, 8 * g + 8)
-        rate, gain = scan_w_ref[0, part, :], gain_ref[part, :]
-        next_columns = []
-        for y in range(2):
-            columns = slice(y * LANES, (y + 1) * LANES)
-            j = 2 * (y * groups + g)
+        mom[y, r] = packed
+
+        def send_moments(i, c):
+            pltpu.make_async_remote_copy(
+                src_ref=mom.at[y, r], dst_ref=mom.at[y, r],
+                send_sem=mom_sem.at[0], recv_sem=mom_sem.at[1 + y],
+                device_id=at(i, 0), device_id_type=MESH,
+            ).start()
+            return c
+
+        lax.fori_loop(1, rows, send_moments, 0)
+        return own_next
+
+    def row_solve(y, own_next):
+        finish(mom.at[y], rows - 1, mom_sem.at[1 + y])
+
+        def gather_moments(i, state):
+            direct, cross = state
+            values = mom[y, lax.rem(r + i, rows)]
+            return direct + direct_ref[i] * values, cross + cross_ref[i] * values
+
+        nothing = jnp.zeros((8, LANES), jnp.float32)
+        direct, cross = lax.fori_loop(0, rows, gather_moments, (nothing, nothing), unroll=UNROLL)
+        inflow = direct + jnp.where(
+            lax.rem(lane8, 2) == 0, pltpu.roll(cross, 1, 1), pltpu.roll(cross, LANES - 1, 1)
+        )
+        for g in range(groups):
+            part = slice(8 * g, 8 * g + 8)
+            j = 2 * g
             west = (j + LANES - 1) % LANES
             from_east = jnp.broadcast_to(inflow[:, j : j + 1], (8, LANES))
             from_west = jnp.broadcast_to(inflow[:, west : west + 1], (8, LANES))
-            onward = pm[part, columns] + phi_w_ref[part, :] * from_west
-            pm[part, columns] = onward + phi_e_ref[part, :] * from_east
-            beyond = rate * jnp.broadcast_to(onward[:, LANES - 1 :], (8, LANES)) + gain * from_east
+            onward = pm[y, part] + phi_w_ref[part, :] * from_west
+            pm[y, part] = onward + phi_e_ref[part, :] * from_east
+            beyond = (
+                scan_w_ref[0, part, :] * jnp.broadcast_to(onward[:, LANES - 1 :], (8, LANES))
+                + gain_ref[part, :] * from_east
+            )
             if g == 0:
                 beyond = jnp.where(
-                    sub8 == 0, own_next[y] + from_west + float(LANES) * from_east, beyond
+                    sub8 == 0, own_next + from_west + float(LANES) * from_east, beyond
                 )
-            next_columns.append(beyond)
-        extra[part, :] = jnp.where(lane8 == 0, next_columns[0], next_columns[1])
-
-    beyond = jnp.dot(
-        jnp.transpose(extra[...])[0:8], cosine_ref[...],
-        precision=HIGHEST, preferred_element_type=jnp.float32,
-    )
-    solved = jnp.dot(cosine_t_ref[...], pm[...], precision=HIGHEST, preferred_element_type=jnp.float32)
-    tall = levels_here + 4
-    for to in range(heights):
-        z0 = to * levels_here
-        half = z0 // LANES
-        for y in range(2):
-            base = (2 * to + y) * tall
-            columns = slice(y * LANES, (y + 1) * LANES)
+            extra[part, :] = beyond
+        solved = jnp.dot(
+            cosine_t_ref[...], pm[y], precision=HIGHEST, preferred_element_type=jnp.float32
+        )
+        beyond = jnp.dot(
+            jnp.transpose(extra[...])[0:8], cosine_ref[...],
+            precision=HIGHEST, preferred_element_type=jnp.float32,
+        )
+        for to in range(heights):
+            z0 = to * levels_here
+            half = z0 // LANES
             top = min(z0 + levels_here, nz - 1)
-            p_out[base : base + levels_here] = solved[z0 : z0 + levels_here, columns]
-            p_out[base + levels_here : base + levels_here + 1] = solved[top : top + 1, columns]
-            p_out[base + levels_here + 1 : base + levels_here + 2] = beyond[
-                y : y + 1, half * LANES : (half + 1) * LANES
+            p_out[y, to, 0:levels_here] = solved[z0 : z0 + levels_here]
+            p_out[y, to, levels_here : levels_here + 1] = solved[top : top + 1]
+            p_out[y, to, levels_here + 1 : levels_here + 2] = beyond[
+                0:1, half * LANES : (half + 1) * LANES
             ]
 
-    def send_back(i, c):
-        to = lax.rem(h + i, heights)
-        pltpu.make_async_remote_copy(
-            src_ref=p_out.at[pl.ds(to * 2 * tall, 2 * tall)],
-            dst_ref=p_in.at[pl.ds(h * 2 * tall, 2 * tall)],
-            send_sem=back_sem.at[0], recv_sem=back_sem.at[1],
-            device_id=(r, to), device_id_type=MESH,
-        ).start()
-        return c
-
-    lax.fori_loop(1, heights, send_back, 0)
-    mine = pl.ds(h * 2 * tall, 2 * tall)
-    own_block = pltpu.make_async_copy(p_out.at[mine], p_in.at[mine], out_sem.at[3])
-    own_block.start()
+        def send_back(i, c):
+            to = lax.rem(h + i, heights)
+            pltpu.make_async_remote_copy(
+                src_ref=p_out.at[y, to, pl.ds(0, TALL)],
+                dst_ref=p_in.at[2 * h + y, pl.ds(0, TALL)],
+                send_sem=back_sem.at[0], recv_sem=back_sem.at[1],
+                device_id=(r, to), device_id_type=MESH,
+            ).start()
+            return c
+
+        lax.fori_loop(1, heights, send_back, 0)
+        own_block = pltpu.make_async_copy(
+            p_out.at[y, h, pl.ds(0, TALL)], p_in.at[2 * h + y, pl.ds(0, TALL)], out_sem.at[3 + y]
+        )
+        own_block.start()
+        return own_block
+
+    own_next = [row_scans(0), row_scans(1)]
+    own_blocks = [row_solve(0, own_next[0]), row_solve(1, own_next[1])]
     finish(d_out, (heights - 1) * block, a2a_sem.at[0])
-    finish(mom, rows - 1, mom_sem.at[0])
+    part = mom.at[:, pl.ds(0, rows - 1)]
+    pltpu.make_async_copy(part, part, mom_sem.at[0]).wait()
     warm_out.wait()
-    for copy in star_out:
+    for copy in star_out + own_blocks:
         copy.wait()
-    own_block.wait()
-    finish(p_in, (heights - 1) * 2 * tall, back_sem.at[1])
-    finish(p_out, (heights - 1) * 2 * tall, back_sem.at[0])
+    for sem in (back_sem.at[1], back_sem.at[0]):
+        part = p_in.at[pl.ds(0, 2 * (heights - 1)), pl.ds(0, TALL)]
+        pltpu.make_async_copy(part, part, sem).wait()
 
 
 def project_kernel(
@@ -477,7 +481,7 @@
         load.start()
     h = lax.axis_index("height")
     levels_here, planes = us.shape[0], us.shape[1]
-    tall = levels_here + 4
+    tall = SLOT
     lane = lax.broadcasted_iota(jnp.int32, (planes, LANES), 1)
     loads[0].wait()
     warm_out = pltpu.make_async_copy(warm, tn_hbm, out_sem.at[2])
@@ -522,7 +526,7 @@
         dma = pltpu.SemaphoreType.DMA
         call = pl.pallas_call(
             functools.partial(kernel, rows, heights),
-            out_shape=(field, field, jax.ShapeDtypeStruct((2 * heights * (levels_here + 4), LANES), f32), field),
+            out_shape=(field, field, jax.ShapeDtypeStruct((planes, SLOT, LANES), f32), field),
             in_specs=[hbm] * 6 + [smem] * 2 + [hbm] * 11,
             out_specs=(hbm,) * 4,
             scratch_shapes=[
@@ -554,13 +558,13 @@
                 pltpu.VMEM(u.shape, f32),
                 pltpu.VMEM(u.shape, f32),
                 pltpu.VMEM((2 * nz, LANES), f32),
-                pltpu.VMEM((2 * nz, LANES), f32),
-                pltpu.VMEM((nz, 2 * LANES), f32),
+                pltpu.VMEM((2, nz, LANES), f32),
+                pltpu.VMEM((2, nz, LANES), f32),
                 pltpu.VMEM((nz, LANES), f32),
-                pltpu.VMEM((rows, 8, LANES), f32),
-                pltpu.VMEM((2 * heights * (levels_here + 4), LANES), f32),
-                dma((3,)), dma((14,)), dma((4,)), dma((2, 3)), dma((2, 5)), dma((2, 2)),
-                dma((2,)), dma((2,)), dma((2,)),
+                pltpu.VMEM((2, rows, 8, LANES), f32),
+                pltpu.VMEM((2, heights, SLOT, LANES), f32),
+                dma((3,)), dma((14,)), dma((5,)), dma((2, 3)), dma((2, 5)), dma((2, 2)),
+                dma((3,)), dma((3,)), dma((2,)),
             ],
             compiler_params=pltpu.CompilerParams(
                 collective_id=0, has_side_effects=True, vmem_limit_bytes=60 * 1024 * 1024
@@ -578,13 +582,13 @@
             in_specs=[hbm] * 4,
             out_specs=(hbm,) * 3,
             scratch_shapes=[
-                pltpu.VMEM(u.shape, f32), pltpu.VMEM(u.shape, f32), pltpu.VMEM(p.shape, f32),
+                pltpu.VMEM(u.shape, f32), pltpu.VMEM(u.shape, f32), pltpu.VMEM((planes * SLOT, LANES), f32),
                 pltpu.VMEM(u.shape, f32), pltpu.VMEM(u.shape, f32), pltpu.VMEM(u.shape, f32),
                 dma((4,)), dma((3,)),
             ],
             compiler_params=pltpu.CompilerParams(vmem_limit_bytes=60 * 1024 * 1024),
         )
-        return project(us, ws, p, warm)
+        return project(us, ws, p.reshape(planes * SLOT, LANES), warm)
 
     field = P("height", None, "row")
     line = P(None, "row")

time: 53.7 us -> 51.4 us (0.957)
  Pallas kernels: 52.9 us -> 50.5 us
    pallas_call x1, Pallas kernels: 50.6 us -> 48.3 us  [per_device(): call(u, w, t, classes, paved, sun, lookup, table['haze'], table['cosine']...]
where the time goes in v4:
time: 51.4 us; the launch traced here: 51.2 us
  Pallas kernels  50.5 us (98%)
  between operations  0.64 us (1%)
    pallas_call x1, Pallas kernels, per_device(): call(u, w, t, classes, paved, sun, lookup, table['haze'], table['cosine']...  48.3 us
    pallas_call x1, Pallas kernels, per_device(): return project(us, ws, p.reshape(planes * SLOT, LANES), warm)  2.28 us

profile of v4, /device:TPU:1, one launch (start us, length us, event | category | flops | bytes accessed | tf_op | source)
XLA Modules:
  0.0 51.2 jit_solution(3000318677656984469)
XLA Ops:
  0.6 48.3 %shard_map.202 = (f32[16,32,128]{2,1,0:T(8,128)}, f32[16,32,128]{2,1,0:T(8,128)}, f32[32,24,128]{2,1,0:T(8,128)}, f32[16,32,128]{2,1,0:T(8,128)}) custom-call(f32[16,32,128]{2,1,0:T(8,128)} %u_hbm.1, f32[16,32,128]{2,1,0:T(8,128)} %w_hbm.1, f32[16,32,128]{2,1,0:T(8,128)} %t_hbm.1, s32[16,32,128]{2,1,0:T(8,128)} %class_hbm.1, s32[32,128]{1,0:T(8,128)} %paved_hbm.1, ...), custom_call_target="tpu_custom_call" | custom-call | tf_op jit(solution)/shard_map/pallas_call | solution.py:573
  48.9 2.3 %shard_map.203 = (f32[16,32,128]{2,1,0:T(8,128)}, f32[16,32,128]{2,1,0:T(8,128)}, f32[16,32,128]{2,1,0:T(8,128)}) custom-call(f32[16,32,128]{2,1,0:T(8,128)} %get-tuple-element.7.us_hbm, f32[16,32,128]{2,1,0:T(8,128)} %get-tuple-element.8.ws_hbm, f32[768,128]{1,0:T(8,128)} %bitcast.1, f32[16,32,128]{2,1,0:T(8,128)} %get-tuple-element.10.warm_hbm), custom_call_target="tpu_custom_call" | custom-call | tf_op jit(solution)/shard_map/pallas_call | solution.py:591

commit v5 on v4

--- a/solution.py
+++ b/solution.py
@@ -106,6 +106,29 @@
     def at(dr, dh):
         return (lax.rem(r + dr + rows, rows), lax.rem(h + dh + heights, heights))
 
+    depth = 8 if rows % 8 == 0 else rows
+    wide = rows // depth
+    x_of, z_of = lax.div(r, depth), lax.rem(r, depth)
+
+    def outward(i, count):
+        return count // 2 + ((i + 1) // 2) * (1 - 2 * (i % 2))
+
+    def row_peer(i):
+        x = lax.rem(x_of + outward(i // depth, wide), wide)
+        return (x * depth + lax.rem(z_of + outward(i % depth, depth), depth), h)
+
+    def height_peer(i):
+        return lax.rem(h + outward(i, heights), heights)
+
+    barrier = pltpu.get_barrier_semaphore()
+
+    for i in range(rows - 1):
+        pl.semaphore_signal(barrier, inc=1, device_id=row_peer(i), device_id_type=MESH)
+    for i in range(heights - 1):
+        pl.semaphore_signal(barrier, inc=1, device_id=(r, height_peer(i)), device_id_type=MESH)
+    corners = (at(1, 1), at(1, -1), at(-1, 1))
+    for corner in (*corners, at(-1, -1)):
+        pl.semaphore_signal(barrier, inc=1, device_id=corner, device_id_type=MESH)
     first_class = pltpu.make_async_copy(class_hbm, class_ref, other_sem.at[0])
     loads = [
         pltpu.make_async_copy(ref, ext.at[f, pl.ds(1, levels_here)], in_sem.at[f])
@@ -124,22 +147,6 @@
             (cosine_t_hbm, cosine_t_ref),
         ))
     ]
-
-    barrier = pltpu.get_barrier_semaphore()
-
-    def greet_height(i, c):
-        pl.semaphore_signal(barrier, inc=1, device_id=at(0, i), device_id_type=MESH)
-        return c
-
-    def greet_row(i, c):
-        pl.semaphore_signal(barrier, inc=1, device_id=at(i, 0), device_id_type=MESH)
-        return c
-
-    lax.fori_loop(1, heights, greet_height, 0)
-    lax.fori_loop(1, rows, greet_row, 0)
-    corners = (at(1, 1), at(1, -1), at(-1, 1))
-    for corner in (*corners, at(-1, -1)):
-        pl.semaphore_signal(barrier, inc=1, device_id=corner, device_id_type=MESH)
     for copy in others:
         copy.start()
     for load in loads:
@@ -285,17 +292,14 @@
 
     for y in range(2):
 
-        def send_plane(i, c, y=y):
-            to = lax.rem(h + i, heights)
+        for i in range(heights - 1):
+            to = height_peer(i)
             pltpu.make_async_remote_copy(
                 src_ref=d_out.at[pl.ds((2 * to + y) * levels_here, levels_here)],
                 dst_ref=d_in.at[y, pl.ds(h * levels_here, levels_here)],
                 send_sem=a2a_sem.at[0], recv_sem=a2a_sem.at[1 + y],
                 device_id=(r, to), device_id_type=MESH,
             ).start()
-            return c
-
-        lax.fori_loop(1, heights, send_plane, 0)
     for y in range(2):
         d_in[y, pl.ds(h * levels_here, levels_here)] = d_out[
             pl.ds((2 * h + y) * levels_here, levels_here)
@@ -381,15 +385,12 @@
                 packed = jnp.where(mine, turned, packed)
         mom[y, r] = packed
 
-        def send_moments(i, c):
+        for i in range(rows - 1):
             pltpu.make_async_remote_copy(
                 src_ref=mom.at[y, r], dst_ref=mom.at[y, r],
                 send_sem=mom_sem.at[0], recv_sem=mom_sem.at[1 + y],
-                device_id=at(i, 0), device_id_type=MESH,
+                device_id=row_peer(i), device_id_type=MESH,
             ).start()
-            return c
-
-        lax.fori_loop(1, rows, send_moments, 0)
         return own_next
 
     def row_solve(y, own_next):
@@ -439,17 +440,14 @@
                 0:1, half * LANES : (half + 1) * LANES
             ]
 
-        def send_back(i, c):
-            to = lax.rem(h + i, heights)
+        for i in range(heights - 1):
+            to = height_peer(i)
             pltpu.make_async_remote_copy(
                 src_ref=p_out.at[y, to, pl.ds(0, TALL)],
                 dst_ref=p_in.at[2 * h + y, pl.ds(0, TALL)],
                 send_sem=back_sem.at[0], recv_sem=back_sem.at[1],
                 device_id=(r, to), device_id_type=MESH,
             ).start()
-            return c
-
-        lax.fori_loop(1, heights, send_back, 0)
         own_block = pltpu.make_async_copy(
             p_out.at[y, h, pl.ds(0, TALL)], p_in.at[2 * h + y, pl.ds(0, TALL)], out_sem.at[3 + y]
         )

time: 51.4 us -> 48.9 us (0.951)
  Pallas kernels: 50.5 us -> 48.1 us
    pallas_call x1, Pallas kernels: 48.3 us -> 45.8 us  [per_device(): call(u, w, t, classes, paved, sun, lookup, table['haze'], table['cosine']...]
where the time goes in v5:
time: 48.9 us; the launch traced here: 48.7 us
  Pallas kernels  48.1 us (98%)
  between operations  0.64 us (1%)
    pallas_call x1, Pallas kernels, per_device(): call(u, w, t, classes, paved, sun, lookup, table['haze'], table['cosine']...  45.8 us
    pallas_call x1, Pallas kernels, per_device(): return project(us, ws, p.reshape(planes * SLOT, LANES), warm)  2.28 us

profile of v5, /device:TPU:1, one launch (start us, length us, event | category | flops | bytes accessed | tf_op | source)
XLA Modules:
  0.0 48.7 jit_solution(10468181245857302061)
XLA Ops:
  0.6 45.8 %shard_map.202 = (f32[16,32,128]{2,1,0:T(8,128)}, f32[16,32,128]{2,1,0:T(8,128)}, f32[32,24,128]{2,1,0:T(8,128)}, f32[16,32,128]{2,1,0:T(8,128)}) custom-call(f32[16,32,128]{2,1,0:T(8,128)} %u_hbm.1, f32[16,32,128]{2,1,0:T(8,128)} %w_hbm.1, f32[16,32,128]{2,1,0:T(8,128)} %t_hbm.1, s32[16,32,128]{2,1,0:T(8,128)} %class_hbm.1, s32[32,128]{1,0:T(8,128)} %paved_hbm.1, ...), custom_call_target="tpu_custom_call" | custom-call | tf_op jit(solution)/shard_map/pallas_call | solution.py:571
  46.4 2.3 %shard_map.203 = (f32[16,32,128]{2,1,0:T(8,128)}, f32[16,32,128]{2,1,0:T(8,128)}, f32[16,32,128]{2,1,0:T(8,128)}) custom-call(f32[16,32,128]{2,1,0:T(8,128)} %get-tuple-element.7.us_hbm, f32[16,32,128]{2,1,0:T(8,128)} %get-tuple-element.8.ws_hbm, f32[768,128]{1,0:T(8,128)} %bitcast.1, f32[16,32,128]{2,1,0:T(8,128)} %get-tuple-element.10.warm_hbm), custom_call_target="tpu_custom_call" | custom-call | tf_op jit(solution)/shard_map/pallas_call | solution.py:589

commit v6 on v5

--- a/solution.py
+++ b/solution.py
@@ -85,14 +85,13 @@
     u_hbm, w_hbm, t_hbm, class_hbm, paved_hbm, sun_hbm, lookup_ref, haze_ref,
     cosine_hbm, cosine_t_hbm, scan_e_hbm, scan_w_hbm, gain_hbm, phi_w_hbm, phi_e_hbm, near_hbm,
     near_next_hbm, direct_hbm, cross_hbm,
-    us_hbm, ws_hbm, p_in, tn_hbm,
+    us, ws, p_in, tn_ref,
     class_ref, paved_ref, sun_ref,
     cosine_ref, cosine_t_ref, scan_e_ref, scan_w_ref, gain_ref, phi_w_ref, phi_e_ref, near_ref,
     near_next_ref, direct_ref, cross_ref,
-    tn_ref,
-    ext, leaf, leaf_sum, leaf_in, low_out, low_in, side_out, side_in, side, u_side, us, ws,
+    ext, leaf, leaf_sum, leaf_in, low_out, low_in, side_out, side_in, side, u_side,
     d_out, d_in, pm, extra, mom, p_out,
-    in_sem, other_sem, out_sem,
+    in_sem, other_sem,
     z_sem, side_sem, leaf_sem, a2a_sem, mom_sem, back_sem,
 ):
     r = lax.axis_index("row")
@@ -304,12 +303,6 @@
         d_in[y, pl.ds(h * levels_here, levels_here)] = d_out[
             pl.ds((2 * h + y) * levels_here, levels_here)
         ]
-    star_out = [
-        pltpu.make_async_copy(us, us_hbm, out_sem.at[0]),
-        pltpu.make_async_copy(ws, ws_hbm, out_sem.at[1]),
-    ]
-    for copy in star_out:
-        copy.start()
     for copy in others[:2]:
         copy.wait()
 
@@ -334,8 +327,6 @@
         return over, bottom
 
     lax.fori_loop(0, levels_here, heat, (over, first), unroll=UNROLL)
-    warm_out = pltpu.make_async_copy(tn_ref, tn_hbm, out_sem.at[2])
-    warm_out.start()
     for copy in others[2:]:
         copy.wait()
 
@@ -364,17 +355,8 @@
             ends = jnp.where(lane_c == 0, bwd, fwd)
             if start == 0:
                 zero = d[0:8]
-                own = jnp.dot(
-                    zero, near_ref[...], precision=HIGHEST, preferred_element_type=jnp.float32
-                )
-                own_next = jnp.dot(
-                    zero, near_next_ref[...], precision=HIGHEST, preferred_element_type=jnp.float32
-                )
                 first_moment = jnp.sum(zero * lane8.astype(jnp.float32), axis=1, keepdims=True)
-                pm[y, 0:8] = jnp.where(sub8 == 0, own, local[0:8])
-                pm[y, 8:chunk] = local[8:]
-            else:
-                pm[y, part] = local
+            pm[y, part] = local
             for i in range(chunk // 8):
                 value = ends[8 * i : 8 * i + 8]
                 if start == 0 and i == 0:
@@ -391,7 +373,11 @@
                 send_sem=mom_sem.at[0], recv_sem=mom_sem.at[1 + y],
                 device_id=row_peer(i), device_id_type=MESH,
             ).start()
-        return own_next
+        own = jnp.dot(zero, near_ref[...], precision=HIGHEST, preferred_element_type=jnp.float32)
+        pm[y, 0:8] = jnp.where(sub8 == 0, own, pm[y, 0:8])
+        return jnp.dot(
+            zero, near_next_ref[...], precision=HIGHEST, preferred_element_type=jnp.float32
+        )
 
     def row_solve(y, own_next):
         finish(mom.at[y], rows - 1, mom_sem.at[1 + y])
@@ -448,62 +434,50 @@
                 send_sem=back_sem.at[0], recv_sem=back_sem.at[1],
                 device_id=(r, to), device_id_type=MESH,
             ).start()
-        own_block = pltpu.make_async_copy(
-            p_out.at[y, h, pl.ds(0, TALL)], p_in.at[2 * h + y, pl.ds(0, TALL)], out_sem.at[3 + y]
-        )
-        own_block.start()
-        return own_block
+        p_in[2 * h + y] = p_out[y, h]
 
     own_next = [row_scans(0), row_scans(1)]
-    own_blocks = [row_solve(0, own_next[0]), row_solve(1, own_next[1])]
+    for y in range(2):
+        row_solve(y, own_next[y])
     finish(d_out, (heights - 1) * block, a2a_sem.at[0])
     part = mom.at[:, pl.ds(0, rows - 1)]
     pltpu.make_async_copy(part, part, mom_sem.at[0]).wait()
-    warm_out.wait()
-    for copy in star_out + own_blocks:
-        copy.wait()
     for sem in (back_sem.at[1], back_sem.at[0]):
         part = p_in.at[pl.ds(0, 2 * (heights - 1)), pl.ds(0, TALL)]
         pltpu.make_async_copy(part, part, sem).wait()
 
 
 def project_kernel(
-    heights, us_hbm, ws_hbm, p_hbm, warm_hbm, un_hbm, wn_hbm, tn_hbm,
-    us, ws, p_in, warm, un, wn, in_sem, out_sem,
+    heights, us, ws, p_in, warm, un_hbm, wn_hbm, tn_hbm, un, wn, out_sem,
 ):
-    loads = [
-        pltpu.make_async_copy(src, dst, in_sem.at[i])
-        for i, (src, dst) in enumerate(((warm_hbm, warm), (p_hbm, p_in), (us_hbm, us), (ws_hbm, ws)))
-    ]
-    for load in loads:
-        load.start()
+    warm_out = pltpu.make_async_copy(warm, tn_hbm, out_sem.at[4])
+    warm_out.start()
     h = lax.axis_index("height")
     levels_here, planes = us.shape[0], us.shape[1]
-    tall = SLOT
     lane = lax.broadcasted_iota(jnp.int32, (planes, LANES), 1)
-    loads[0].wait()
-    warm_out = pltpu.make_async_copy(warm, tn_hbm, out_sem.at[2])
-    warm_out.start()
-    for load in loads[1:]:
-        load.wait()
-    beyond = p_in[pl.ds(levels_here + 1, planes, stride=tall), :]
+    beyond = p_in[pl.ds(levels_here + 1, planes, stride=SLOT), :]
     first = lax.rem(h * levels_here, LANES)
 
     def project(z, p):
         edge = pltpu.roll(beyond, LANES - 1 - first - z, 1)
         east = jnp.where(lane == LANES - 1, edge, pltpu.roll(p, LANES - 1, 1))
         un[z] = us[z] - (east - p)
-        above = p_in[pl.ds(z + 1, planes, stride=tall), :]
+        above = p_in[pl.ds(z + 1, planes, stride=SLOT), :]
         wn[z] = ws[z] - (above - p)
         return above
 
-    lax.fori_loop(0, levels_here, project, p_in[pl.ds(0, planes, stride=tall), :], unroll=UNROLL)
-    stores = [
-        pltpu.make_async_copy(un, un_hbm, out_sem.at[0]),
-        pltpu.make_async_copy(wn, wn_hbm, out_sem.at[1]),
-    ]
-    for store in stores:
-        store.start()
+    p = p_in[pl.ds(0, planes, stride=SLOT), :]
+    half = levels_here // 2
+    stores = []
+    for part in range(2):
+        p = lax.fori_loop(part * half, part * half + half, project, p, unroll=UNROLL)
+        rows_here = pl.ds(part * half, half)
+        for i, (src, dst) in enumerate(((un, un_hbm), (wn, wn_hbm))):
+            store = pltpu.make_async_copy(
+                src.at[rows_here], dst.at[rows_here], out_sem.at[2 * part + i]
+            )
+            store.start()
+            stores.append(store)
     warm_out.wait()
     for store in stores:
         store.wait()
@@ -517,7 +491,8 @@
         nz = levels_here * heights
         table = tables(nz, width * rows, rows)
         smem = pl.BlockSpec(memory_space=pltpu.SMEM)
-        hbm = pl.BlockSpec(memory_space=pl.ANY)
+        hbm = pl.BlockSpec(memory_space=pltpu.HBM)
+        vmem = pl.BlockSpec(memory_space=pltpu.VMEM)
         field = jax.ShapeDtypeStruct(u.shape, jnp.float32)
         plane = (planes, LANES)
         f32 = jnp.float32
@@ -526,7 +501,7 @@
             functools.partial(kernel, rows, heights),
             out_shape=(field, field, jax.ShapeDtypeStruct((planes, SLOT, LANES), f32), field),
             in_specs=[hbm] * 6 + [smem] * 2 + [hbm] * 11,
-            out_specs=(hbm,) * 4,
+            out_specs=(vmem,) * 4,
             scratch_shapes=[
                 pltpu.VMEM((levels_here,) + plane, jnp.int32),
                 pltpu.VMEM(plane, jnp.int32),
@@ -542,7 +517,6 @@
                 pltpu.VMEM((LANES, LANES), f32),
                 pltpu.VMEM((rows, 8, LANES), f32),
                 pltpu.VMEM((rows, 8, LANES), f32),
-                pltpu.VMEM(u.shape, f32),
                 pltpu.VMEM((3, levels_here + 2) + plane, f32),
                 pltpu.VMEM((levels_here,) + plane, f32),
                 pltpu.VMEM(plane, f32),
@@ -553,20 +527,23 @@
                 pltpu.VMEM((5,) + plane, f32),
                 pltpu.VMEM(plane, f32),
                 pltpu.VMEM(plane, f32),
-                pltpu.VMEM(u.shape, f32),
-                pltpu.VMEM(u.shape, f32),
                 pltpu.VMEM((2 * nz, LANES), f32),
                 pltpu.VMEM((2, nz, LANES), f32),
                 pltpu.VMEM((2, nz, LANES), f32),
                 pltpu.VMEM((nz, LANES), f32),
                 pltpu.VMEM((2, rows, 8, LANES), f32),
                 pltpu.VMEM((2, heights, SLOT, LANES), f32),
-                dma((3,)), dma((14,)), dma((5,)), dma((2, 3)), dma((2, 5)), dma((2, 2)),
+                dma((3,)), dma((14,)), dma((2, 3)), dma((2, 5)), dma((2, 2)),
                 dma((3,)), dma((3,)), dma((2,)),
             ],
             compiler_params=pltpu.CompilerParams(
-                collective_id=0, has_side_effects=True, vmem_limit_bytes=60 * 1024 * 1024
+                collective_id=0, has_side_effects=True, vmem_limit_bytes=24 * 1024 * 1024
             ),
+        )
+        stay = lambda a: pltpu.with_memory_space_constraint(jnp.asarray(a), pltpu.HBM)
+        table = {name: stay(values) for name, values in table.items()}
+        u, w, t, classes, paved, sun, lookup = map(
+            stay, (u, w, t, classes, paved, sun, lookup)
         )
         us, ws, p, warm = call(
             u, w, t, classes, paved, sun, lookup, table["haze"], table["cosine"],
@@ -577,14 +554,10 @@
         project = pl.pallas_call(
             functools.partial(project_kernel, heights),
             out_shape=(field, field, field),
-            in_specs=[hbm] * 4,
+            in_specs=[vmem] * 4,
             out_specs=(hbm,) * 3,
-            scratch_shapes=[
-                pltpu.VMEM(u.shape, f32), pltpu.VMEM(u.shape, f32), pltpu.VMEM((planes * SLOT, LANES), f32),
-                pltpu.VMEM(u.shape, f32), pltpu.VMEM(u.shape, f32), pltpu.VMEM(u.shape, f32),
-                dma((4,)), dma((3,)),
-            ],
-            compiler_params=pltpu.CompilerParams(vmem_limit_bytes=60 * 1024 * 1024),
+            scratch_shapes=[pltpu.VMEM(u.shape, f32), pltpu.VMEM(u.shape, f32), dma((5,))],
+            compiler_params=pltpu.CompilerParams(vmem_limit_bytes=24 * 1024 * 1024),
         )
         return project(us, ws, p.reshape(planes * SLOT, LANES), warm)
 

time: 48.9 us -> 47.4 us (0.969)
  Pallas kernels: 48.1 us -> 46.6 us
    pallas_call x1, Pallas kernels: 2.28 us -> 0.98 us  [per_device(): return project(us, ws, p.reshape(planes * SLOT, LANES), warm)]
where the time goes in v6:
time: 47.4 us; the launch traced here: 47.2 us
  Pallas kernels  46.6 us (98%)
  between operations  0.64 us (1%)
    pallas_call x1, Pallas kernels, per_device(): call(u, w, t, classes, paved, sun, lookup, table['haze'], table['cosine']...  45.6 us
    pallas_call x1, Pallas kernels, per_device(): return project(us, ws, p.reshape(planes * SLOT, LANES), warm)  0.98 us

profile of v6, /device:TPU:1, one launch (start us, length us, event | category | flops | bytes accessed | tf_op | source)
XLA Modules:
  0.0 47.2 jit_solution(7967968754022134069)
XLA Ops:
  0.6 45.6 %shard_map.202 = (f32[16,32,128]{2,1,0:T(8,128)S(1)}, f32[16,32,128]{2,1,0:T(8,128)S(1)}, f32[32,24,128]{2,1,0:T(8,128)S(1)}, f32[16,32,128]{2,1,0:T(8,128)S(1)}) custom-call(f32[16,32,128]{2,1,0:T(8,128)} %u_hbm.1, f32[16,32,128]{2,1,0:T(8,128)} %w_hbm.1, f32[16,32,128]{2,1,0:T(8,128)} %t_hbm.1, s32[16,32,128]{2,1,0:T(8,128)} %class_hbm.1, ...), custom_call_target="tpu_custom_call" | custom-call | tf_op jit(solution)/shard_map/pallas_call | solution.py:548
  46.3 1.0 %shard_map.203 = (f32[16,32,128]{2,1,0:T(8,128)}, f32[16,32,128]{2,1,0:T(8,128)}, f32[16,32,128]{2,1,0:T(8,128)}) custom-call(f32[16,32,128]{2,1,0:T(8,128)S(1)} %get-tuple-element.7.us, f32[16,32,128]{2,1,0:T(8,128)S(1)} %get-tuple-element.8.ws, f32[768,128]{1,0:T(8,128)S(1)} %bitcast.1, f32[16,32,128]{2,1,0:T(8,128)S(1)} %get-tuple-element.10.warm), custom_call_target="tpu_custom_call" | custom-call | tf_op jit(solution)/shard_map/pallas_call | solution.py:562

commit v7 on v6

--- a/solution.py
+++ b/solution.py
@@ -146,8 +146,6 @@
             (cosine_t_hbm, cosine_t_ref),
         ))
     ]
-    for copy in others:
-        copy.start()
     for load in loads:
         load.wait()
     lane = lax.broadcasted_iota(jnp.int32, (planes, LANES), 1)
@@ -192,6 +190,8 @@
     ]
     for copy in halo:
         copy.start()
+    for copy in others:
+        copy.start()
 
     def leaf_level(z, total):
         area = leaf_of(class_ref[z])
@@ -207,21 +207,6 @@
     for copy in leaf_copies:
         copy.start()
 
-    for copy in halo:
-        copy.wait()
-
-    @pl.when(h == 0)
-    def _():
-        ext[:, 0] = jnp.zeros((3, planes, LANES), jnp.float32)
-
-    @pl.when(h == heights - 1)
-    def _():
-        ext[:, levels_here + 1] = jnp.zeros((3, planes, LANES), jnp.float32)
-
-    even = lax.rem(lane, 2) == 0
-    from_left = side_in[0]
-    side[...] = jnp.where(even, pltpu.roll(side_in[1], LANES - 1, 1), pltpu.roll(from_left, 1, 1))
-
     def stretch(q, u, w, east, west, above, below):
         advect = u * (east - west) * 0.5 + w * (above - below) * 0.5
         diffuse = VISCOSITY * (east + west + above + below - 4.0 * q)
@@ -229,6 +214,32 @@
 
     def drag(area, u, w):
         return DRAG_COEF * area * jnp.sqrt(u * u + w * w + SPAN_VAR)
+
+    still = jnp.zeros((planes, LANES), jnp.float32)
+    for z in range(levels_here):
+        u, w, t = ext[0, z + 1], ext[1, z + 1], ext[2, z + 1]
+        friction = drag(leaf[z], u, w)
+        for f, q, star, lift in ((0, u, us, 0.0), (1, w, ws, THERMAL_LIFT * t)):
+            east = jnp.where(lane == LANES - 1, 0.0, pltpu.roll(q, LANES - 1, 1))
+            west = jnp.where(lane == 0, 0.0, pltpu.roll(q, 1, 1))
+            above = ext[f, z + 2] if z < levels_here - 1 else still
+            below = ext[f, z] if z > 0 else still
+            star[z] = q + DT * (stretch(q, u, w, east, west, above, below) - friction * q + lift)
+
+    for copy in halo:
+        copy.wait()
+
+    @pl.when(h == 0)
+    def _():
+        ext[:, 0] = jnp.zeros((3, planes, LANES), jnp.float32)
+
+    @pl.when(h == heights - 1)
+    def _():
+        ext[:, levels_here + 1] = jnp.zeros((3, planes, LANES), jnp.float32)
+
+    even = lax.rem(lane, 2) == 0
+    from_left = side_in[0]
+    side[...] = jnp.where(even, pltpu.roll(side_in[1], LANES - 1, 1), pltpu.roll(from_left, 1, 1))
 
     last = 2 * (levels_here - 1)
     w_left = pltpu.roll(from_left, LANES - 2 * levels_here, 1)
@@ -268,22 +279,30 @@
         west = jnp.where(lane == 0, edge, pltpu.roll(q, 1, 1))
         return stretch(q, u, w, east, west, ext[f, z + 2], ext[f, z])
 
-    def winds(z, w_below):
-        u = ext[0, z + 1]
-        w = ext[1, z + 1]
-        t = ext[2, z + 1]
-        friction = drag(leaf[z], u, w)
-        u_star = u + DT * (growth(0, z, u, w) - friction * u)
-        w_star = w + DT * (growth(1, z, u, w) - friction * w + THERMAL_LIFT * t)
-        w_star = jnp.where(h * levels_here + z == nz - 1, 0.0, w_star)
+    w_below = w_star_low
+    for z in range(levels_here):
+        u, w = ext[0, z + 1], ext[1, z + 1]
+        sides = jnp.where(
+            lane == 0, VISCOSITY + 0.5 * u, jnp.where(lane == LANES - 1, VISCOSITY - 0.5 * u, 0.0)
+        )
+        stars = []
+        for f, star in ((0, us), (1, ws)):
+            edge = pltpu.roll(side[...], LANES - 1 - 2 * (f * levels_here + z), 1)
+            share = sides * edge
+            if z == 0:
+                share = share + (VISCOSITY + 0.5 * w) * ext[f, 0]
+            if z == levels_here - 1:
+                share = share + (VISCOSITY - 0.5 * w) * ext[f, levels_here + 1]
+            stars.append(star[z] + DT * share)
+        u_star, w_star = stars
+        if z == levels_here - 1:
+            w_star = jnp.where(h == heights - 1, 0.0, w_star)
         us[z] = u_star
         ws[z] = w_star
-        edge = pltpu.roll(u_side[...], lax.rem(LANES - 2 * z, LANES), 1)
+        edge = pltpu.roll(u_side[...], (LANES - 2 * z) % LANES, 1)
         west = jnp.where(lane == 0, edge, pltpu.roll(u_star, 1, 1))
         d_out[pl.ds(z, planes, stride=levels_here), :] = u_star - west + (w_star - w_below)
-        return w_star
-
-    lax.fori_loop(0, levels_here, winds, w_star_low, unroll=UNROLL)
+        w_below = w_star
 
     def finish(buffer, count, sem):
         part = buffer.at[pl.ds(0, count)]

time: 47.4 us -> 46.8 us (0.987)
  Pallas kernels: 46.6 us -> 46 us
    pallas_call x1, Pallas kernels: 45.6 us -> 45 us  [per_device(): call(u, w, t, classes, paved, sun, lookup, table['haze'], table['cosine']...]
where the time goes in v7:
time: 46.8 us; the launch traced here: 46.7 us
  Pallas kernels  46 us (98%)
  between operations  0.64 us (1%)
    pallas_call x1, Pallas kernels, per_device(): call(u, w, t, classes, paved, sun, lookup, table['haze'], table['cosine']...  45 us
    pallas_call x1, Pallas kernels, per_device(): return project(us, ws, p.reshape(planes * SLOT, LANES), warm)  0.98 us

profile of v7, /device:TPU:1, one launch (start us, length us, event | category | flops | bytes accessed | tf_op | source)
XLA Modules:
  0.0 46.7 jit_solution(15662381333198279048)
XLA Ops:
  0.6 45.0 %shard_map.202 = (f32[16,32,128]{2,1,0:T(8,128)S(1)}, f32[16,32,128]{2,1,0:T(8,128)S(1)}, f32[32,24,128]{2,1,0:T(8,128)S(1)}, f32[16,32,128]{2,1,0:T(8,128)S(1)}) custom-call(f32[16,32,128]{2,1,0:T(8,128)} %u_hbm.1, f32[16,32,128]{2,1,0:T(8,128)} %w_hbm.1, f32[16,32,128]{2,1,0:T(8,128)} %t_hbm.1, s32[16,32,128]{2,1,0:T(8,128)} %class_hbm.1, ...), custom_call_target="tpu_custom_call" | custom-call | tf_op jit(solution)/shard_map/pallas_call | solution.py:567
  45.7 1.0 %shard_map.203 = (f32[16,32,128]{2,1,0:T(8,128)}, f32[16,32,128]{2,1,0:T(8,128)}, f32[16,32,128]{2,1,0:T(8,128)}) custom-call(f32[16,32,128]{2,1,0:T(8,128)S(1)} %get-tuple-element.7.us, f32[16,32,128]{2,1,0:T(8,128)S(1)} %get-tuple-element.8.ws, f32[768,128]{1,0:T(8,128)S(1)} %bitcast.1, f32[16,32,128]{2,1,0:T(8,128)S(1)} %get-tuple-element.10.warm), custom_call_target="tpu_custom_call" | custom-call | tf_op jit(solution)/shard_map/pallas_call | solution.py:581

commit v8 on v7

--- a/solution.py
+++ b/solution.py
@@ -119,15 +119,6 @@
     def height_peer(i):
         return lax.rem(h + outward(i, heights), heights)
 
-    barrier = pltpu.get_barrier_semaphore()
-
-    for i in range(rows - 1):
-        pl.semaphore_signal(barrier, inc=1, device_id=row_peer(i), device_id_type=MESH)
-    for i in range(heights - 1):
-        pl.semaphore_signal(barrier, inc=1, device_id=(r, height_peer(i)), device_id_type=MESH)
-    corners = (at(1, 1), at(1, -1), at(-1, 1))
-    for corner in (*corners, at(-1, -1)):
-        pl.semaphore_signal(barrier, inc=1, device_id=corner, device_id_type=MESH)
     first_class = pltpu.make_async_copy(class_hbm, class_ref, other_sem.at[0])
     loads = [
         pltpu.make_async_copy(ref, ext.at[f, pl.ds(1, levels_here)], in_sem.at[f])
@@ -136,6 +127,15 @@
     for load in loads:
         load.start()
     first_class.start()
+    barrier = pltpu.get_barrier_semaphore()
+
+    for i in range(rows - 1):
+        pl.semaphore_signal(barrier, inc=1, device_id=row_peer(i), device_id_type=MESH)
+    for i in range(heights - 1):
+        pl.semaphore_signal(barrier, inc=1, device_id=(r, height_peer(i)), device_id_type=MESH)
+    corners = (at(1, 1), at(1, -1), at(-1, 1))
+    for corner in (*corners, at(-1, -1)):
+        pl.semaphore_signal(barrier, inc=1, device_id=corner, device_id_type=MESH)
     others = [
         pltpu.make_async_copy(src, dst, other_sem.at[i + 1])
         for i, (src, dst) in enumerate((

time: 46.8 us -> 47.1 us (level)
  no operation moved by 1% of the time
where the time goes in v8:
time: 47.1 us; the launch traced here: 46.9 us
  Pallas kernels  46.3 us (98%)
  between operations  0.64 us (1%)
    pallas_call x1, Pallas kernels, per_device(): call(u, w, t, classes, paved, sun, lookup, table['haze'], table['cosine']...  45.3 us
    pallas_call x1, Pallas kernels, per_device(): return project(us, ws, p.reshape(planes * SLOT, LANES), warm)  0.98 us

profile of v8, /device:TPU:1, one launch (start us, length us, event | category | flops | bytes accessed | tf_op | source)
XLA Modules:
  0.0 46.9 jit_solution(14005342993143009789)
XLA Ops:
  0.6 45.3 %shard_map.202 = (f32[16,32,128]{2,1,0:T(8,128)S(1)}, f32[16,32,128]{2,1,0:T(8,128)S(1)}, f32[32,24,128]{2,1,0:T(8,128)S(1)}, f32[16,32,128]{2,1,0:T(8,128)S(1)}) custom-call(f32[16,32,128]{2,1,0:T(8,128)} %u_hbm.1, f32[16,32,128]{2,1,0:T(8,128)} %w_hbm.1, f32[16,32,128]{2,1,0:T(8,128)} %t_hbm.1, s32[16,32,128]{2,1,0:T(8,128)} %class_hbm.1, ...), custom_call_target="tpu_custom_call" | custom-call | tf_op jit(solution)/shard_map/pallas_call | solution.py:567
  45.9 1.0 %shard_map.203 = (f32[16,32,128]{2,1,0:T(8,128)}, f32[16,32,128]{2,1,0:T(8,128)}, f32[16,32,128]{2,1,0:T(8,128)}) custom-call(f32[16,32,128]{2,1,0:T(8,128)S(1)} %get-tuple-element.7.us, f32[16,32,128]{2,1,0:T(8,128)S(1)} %get-tuple-element.8.ws, f32[768,128]{1,0:T(8,128)S(1)} %bitcast.1, f32[16,32,128]{2,1,0:T(8,128)S(1)} %get-tuple-element.10.warm), custom_call_target="tpu_custom_call" | custom-call | tf_op jit(solution)/shard_map/pallas_call | solution.py:581
